TPU v7x, 32 devices: a whole 2x2x4 slice. The times are simulated.
32 devices in a mesh: mem: 4 (over y, x), space: 8 (over z, core).
Axes of the slice: x: 2, y: 2, z: 4, core: 2. Of those that a mesh axis runs over, the one named last changes fastest.
Arguments:
- log_perm: float32 [8, 32, 128, 128], P('mem', 'space'), may hold values from -4 to 4
- saturation: float32 [32, 128, 128], P('space'), may hold values from 0.1 to 0.9
- pressure_init: float32 [32, 128, 128], P('space'), may hold values from -3 to 3
- wells: int32 [64], replicated, may hold values from 0 to 524287
- well_rate: float32 [64], replicated, may hold values from -4 to 4
- obs_index: int32 [512, 8], replicated, may hold values from 0 to 524287, as said below
- obs_weight: float32 [512, 8], replicated, may hold values from -2 to 2
- obs_value: float32 [512], replicated, may hold values from -5 to 5
- obs_var: float32 [512], replicated, may hold values from 0.1 to 1
- noise: float32 [8, 512], replicated, may hold values from -5 to 5
Outputs:
- updated_perm: float32 [8, 32, 128, 128], P(None, 'space', 'mem')
Inputs may be any that keep to these rules, and one draw needn't show every extreme that they name: `obs_index`: observation o reads only cells of the grid row o % 32 along the first dimension.
All inputs are finite; a program needn't handle non-finite values.
Results may differ from a plain program's by a relative error of at most 0.00007.
Values sent between devices are 32-bit elements; how exact they have to be, the bound alone decides.
A program may use at most 128 MiB of HBM per device.

v0:
```python
import jax
import jax.numpy as jnp
from jax import lax
from jax.sharding import PartitionSpec as P

SWEEPS = 6


water_visc = 1.0
oil_visc = 4.0
time_step = 0.1
storage = 1.0
inflation = 4.0


def padded(cells, sides, width):
    for axis, dim in sides:
        count = lax.axis_size(axis)
        ends = count - 1
        head = lax.slice_in_dim(cells, 0, width, axis=dim)
        tail = lax.slice_in_dim(cells, cells.shape[dim] - width, cells.shape[dim], axis=dim)
        cells = jnp.concatenate(
            [
                lax.ppermute(tail, axis, [(i, (i + 1) % count) for i in range(ends)]),
                cells,
                lax.ppermute(head, axis, [((i + 1) % count, i) for i in range(ends)]),
            ],
            axis=dim,
        )
    return cells


def pad_plane(field):
    return jnp.pad(field, ((0, 0), (0, 0), (1, 1), (1, 1)))


def beside_all(field):
    return [
        field[:, 2:, 1:-1, 1:-1],
        field[:, :-2, 1:-1, 1:-1],
        field[:, 1:-1, 2:, 1:-1],
        field[:, 1:-1, :-2, 1:-1],
        field[:, 1:-1, 1:-1, 2:],
        field[:, 1:-1, 1:-1, :-2],
    ]


def middle(field):
    return field[:, 1:-1, 1:-1, 1:-1]


def props(perm, sat):
    water = sat * sat / water_visc
    oil = (1.0 - sat) * (1.0 - sat) / oil_visc
    total = water + oil
    return (perm * total, water / total)


def saturate(perm_pad, sat_pad, press_pad, source):
    lam, frac = props(perm_pad, sat_pad)
    lam_mid, frac_mid, press_mid = (middle(lam), middle(frac), middle(press_pad))
    outflow = jnp.zeros_like(lam_mid)
    for lam_next, frac_next, press_next in zip(
        beside_all(lam), beside_all(frac), beside_all(press_pad)
    ):
        flux = 0.5 * (lam_mid + lam_next) * (press_mid - press_next)
        outflow = outflow + jnp.maximum(flux, 0.0) * frac_mid + jnp.minimum(flux, 0.0) * frac_next
    water = jnp.maximum(source, 0.0) + jnp.minimum(source, 0.0) * frac_mid
    return jnp.clip(middle(sat_pad) + time_step * (water - outflow), 0.0, 1.0)


def pressure(perm_pad, sat_pad, press_pad, source):
    lam, frac = props(perm_pad, sat_pad)
    lam_mid = middle(lam)
    numer = storage * middle(press_pad) + source
    denom = storage + jnp.zeros_like(lam_mid)
    for lam_next, press_next in zip(beside_all(lam), beside_all(press_pad)):
        trans = 0.5 * (lam_mid + lam_next)
        numer = numer + trans * press_next
        denom = denom + trans
    return numer / denom


def sources(wells, well_rate, first_row, rows, ny, nz):
    plane = ny * nz
    well_x = wells // plane
    rest = wells - well_x * plane
    local_x = well_x - first_row
    valid = (local_x >= 0) & (local_x < rows)
    target = jnp.where(valid, local_x * plane + rest, 0)
    field = jnp.zeros((rows * plane,), jnp.float32).at[target].add(jnp.where(valid, well_rate, 0.0))
    return field.reshape(rows, ny, nz)


def body(
    log_perm,
    saturation,
    pressure_init,
    wells,
    well_rate,
    obs_index,
    obs_weight,
    obs_value,
    obs_var,
    noise,
):
    members, width, ny, nz = log_perm.shape
    shape = (members, width, ny, nz)
    perm = jnp.exp(log_perm)
    sat = jnp.broadcast_to(saturation, shape)
    press = jnp.broadcast_to(pressure_init, shape)
    place = lax.axis_index("space")
    total_rows = width * lax.axis_size("space")
    source = sources(wells, well_rate, place * width, width, ny, nz)
    stacked = padded(jnp.stack([perm, sat, press]), (("space", 2),), 2)
    perm_pad = pad_plane(stacked[0])
    sat_ext = stacked[1]
    press_ext = stacked[2]
    source_wide = sources(wells, well_rate, place * width - 1, width + 2, ny, nz)
    rows_wide = place * width - 1 + jnp.arange(width + 2)
    inside = ((rows_wide >= 0) & (rows_wide < total_rows)).astype(jnp.float32)[:, None, None]
    for sweep in range(SWEEPS):
        sat_wide = (
            saturate(perm_pad, pad_plane(sat_ext), pad_plane(press_ext), source_wide) * inside
        )
        press = pressure(
            perm_pad[:, 1:-1], pad_plane(sat_wide), pad_plane(press_ext[:, 1:-1]), source
        )
        if sweep + 1 < SWEEPS:
            stacked = padded(jnp.stack([sat_wide[:, 1:-1], press]), (("space", 2),), 2)
            sat_ext = stacked[0]
            press_ext = stacked[1]
    cells = width * ny * nz
    flat = press.reshape(members, cells)
    local = obs_index - place * cells
    valid = (local >= 0) & (local < cells)
    picked = jnp.take(flat, jnp.where(valid, local, 0), axis=1)
    partial_value = jnp.sum(picked * jnp.where(valid, obs_weight, 0.0)[None], axis=2)
    summed = lax.psum(partial_value, "space")
    predicted = lax.all_gather(summed, "mem", axis=0, tiled=True)
    ensemble = predicted.shape[0]
    high = lax.Precision.HIGHEST
    dev = predicted - jnp.mean(predicted, axis=0, keepdims=True)
    cov = jnp.dot(dev.T, dev, precision=high) / (ensemble - 1) + inflation * jnp.diag(obs_var)
    resid = obs_value[None, :] + jnp.sqrt(inflation * obs_var)[None, :] * noise - predicted
    factor = jnp.linalg.cholesky(cov)
    half = lax.linalg.triangular_solve(factor, resid.T, left_side=True, lower=True)
    solved = lax.linalg.triangular_solve(factor, half, left_side=True, lower=True, transpose_a=True)
    weights = jnp.dot(dev, solved, precision=high) / (ensemble - 1)
    mixing = (
        jnp.eye(ensemble, dtype=jnp.float32) + weights - jnp.mean(weights, axis=0, keepdims=True)
    )
    columns = lax.all_to_all(log_perm, "mem", split_axis=2, concat_axis=0, tiled=True)
    return jnp.tensordot(mixing.T, columns, axes=1, precision=high)


def solution(mesh):
    placed = (
        P("mem", "space", None, None),
        P("space", None, None),
        P("space", None, None),
        P(),
        P(),
        P(),
        P(),
        P(),
        P(),
        P(),
    )
    return jax.shard_map(
        body, mesh=mesh, in_specs=placed, out_specs=P(None, "space", "mem", None), check_vma=False
    )
```

profile of v0, /device:TPU:0, one launch (start us, length us, event | category | flops | bytes accessed | tf_op | source)
XLA Modules:
  0.0 357.0 jit_solution(4685406150334629817)
XLA Ops:
  4.6 3.2 collective-permute-start
  11.3 2.3 collective-permute-done.1
  17.0 3.6 fusion.223
  22.8 11.5 %collective-permute-start.2 = (f32[2,2,2,128,128]{4,3,2,1,0:T(8,128)S(1)}, f32[2,2,2,128,128]{4,3,2,1,0:T(8,128)S(1)}, u32[]{:S(2)}, u32[]{:S(2)}) collective-permute-start(f32[2,2,2,128,128]{4,3,2,1,0:T(8,128)S(1)} %get-tuple-element.60), channel_id=1, source_target_pairs={{0,1},{1,2},{2,3},{3,4},{4,5},{5,6},{6,7},{8,9},{9,10},{10,11},{11... | collective-permute-start | bytes 1572872 | tf_op jit(solution)/shard_map/ppermute | solution.py:24
  35.8 2.3 collective-permute-done.3
  40.0 3.6 fusion.199
  45.8 8.6 %collective-permute-start.4 = (f32[2,2,2,128,128]{4,3,2,1,0:T(8,128)S(1)}, f32[2,2,2,128,128]{4,3,2,1,0:T(8,128)S(1)}, u32[]{:S(2)}, u32[]{:S(2)}) collective-permute-start(f32[2,2,2,128,128]{4,3,2,1,0:T(8,128)S(1)} %get-tuple-element.56), channel_id=1, source_target_pairs={{0,1},{1,2},{2,3},{3,4},{4,5},{5,6},{6,7},{8,9},{9,10},{10,11},{11... | collective-permute-start | bytes 1572872 | tf_op jit(solution)/shard_map/ppermute | solution.py:24
  55.9 2.3 collective-permute-done.5
  60.1 3.6 fusion.175
  65.9 8.8 %collective-permute-start.6 = (f32[2,2,2,128,128]{4,3,2,1,0:T(8,128)S(1)}, f32[2,2,2,128,128]{4,3,2,1,0:T(8,128)S(1)}, u32[]{:S(2)}, u32[]{:S(2)}) collective-permute-start(f32[2,2,2,128,128]{4,3,2,1,0:T(8,128)S(1)} %get-tuple-element.52), channel_id=1, source_target_pairs={{0,1},{1,2},{2,3},{3,4},{4,5},{5,6},{6,7},{8,9},{9,10},{10,11},{11... | collective-permute-start | bytes 1572872 | tf_op jit(solution)/shard_map/ppermute | solution.py:24
  76.0 2.5 collective-permute-done.7
  80.4 3.6 fusion.151
  87.2 9.4 %collective-permute-start.8 = (f32[2,2,2,128,128]{4,3,2,1,0:T(8,128)}, f32[2,2,2,128,128]{4,3,2,1,0:T(8,128)}, u32[]{:S(2)}, u32[]{:S(2)}) collective-permute-start(f32[2,2,2,128,128]{4,3,2,1,0:T(8,128)} %get-tuple-element.48), channel_id=1, source_target_pairs={{0,1},{1,2},{2,3},{3,4},{4,5},{5,6},{6,7},{8,9},{9,10},{10,11},{11... | collective-permute-start | bytes 1572872 | tf_op jit(solution)/shard_map/ppermute | solution.py:24
  99.0 4.4 %all-to-all-start = ((f32[2,4,128,128]{3,1,0,2:T(4,128)}), f32[2,4,128,128]{3,1,0,2:T(4,128)}, u32[]{:S(2)}, u32[]{:S(2)}) async-start(f32[2,4,128,128]{3,1,0,2:T(4,128)} %copy.32), calls=%async_computation | async-start | bytes 1048576 | tf_op jit(solution)/shard_map/all_to_all | solution.py:153
  107.0 3.6 fusion.127
  113.9 5.2 %collective-permute-start.10 = (f32[2,2,2,128,128]{4,3,2,1,0:T(8,128)}, f32[2,2,2,128,128]{4,3,2,1,0:T(8,128)}, u32[]{:S(2)}, u32[]{:S(2)}) collective-permute-start(f32[2,2,2,128,128]{4,3,2,1,0:T(8,128)} %get-tuple-element.44), channel_id=1, source_target_pairs={{0,1},{1,2},{2,3},{3,4},{4,5},{5,6},{6,7},{8,9},{9,10},{10,11},{11... | collective-permute-start | bytes 1572872 | tf_op jit(solution)/shard_map/ppermute | solution.py:24
  120.9 2.1 copy.33
  126.2 3.6 fusion.103
  131.8 16.4 %copy.27 = f32[2,4,128,128]{0,3,2,1:T(8,128)} copy(f32[2,4,128,128]{3,2,1,0:T(8,128)S(1)} %fusion.297) | data formatting | bytes 1048576 | tf_op jit(solution)/shard_map/div | solution.py:81
  148.2 21.3 %gather_fusion = f32[4096,2]{1,0:T(8,128)S(1)} fusion(f32[2,65536]{0,1:T(8,128)} %bitcast.124, s32[4096]{0:T(1024)S(1)} %broadcast_clamp_fusion), kind=kCustom, calls=%fused_computation | custom fusion | bytes 81920 | tf_op jit(solution)/shard_map/jit(_take)/gather | solution.py:137
  169.6 2.9 fusion.25
  172.4 34.5 %psum.7 = f32[2,512]{0,1:T(8,128)S(1)} all-reduce(f32[2,512]{0,1:T(8,128)S(1)} %bitcast.146), channel_id=1, replica_groups=mesh['mem'=4,'space'=8] {'space'}, use_global_device_ids=true, to_apply=%region_3.4 | all-reduce | flops 1024 | bytes 8192 | tf_op jit(solution)/shard_map/psum | solution.py:139
  207.0 8.6 %all-gather = f32[4,2,512]{2,1,0:T(2,128)S(1)} all-gather(f32[1,2,512]{2,1,0:T(2,128)S(1)} %copy.30), channel_id=1, replica_groups=mesh['mem'=4,'space'=8] {'mem'}, dimensions={0}, use_global_device_ids=true | all-gather | bytes 20480 | tf_op jit(solution)/shard_map/all_gather | solution.py:140
  217.3 11.7 %cholesky.103 = f32[128,128]{1,0:T(8,128)S(1)} custom-call(f32[128,128]{1,0:T(8,128)S(1)} %cholesky.263), custom_call_target="Cholesky" | custom-call | tf_op jit(solution)/shard_map/jit(cholesky)/cholesky | solution.py:146
  229.2 9.8 %custom-call.32 = f32[1,128,128]{1,2,0:T(8,128)S(1)} custom-call(f32[1,128,128]{2,1,0:T(8,128)S(1)} %get-tuple-element.75), custom_call_target="InvertDiagBlocksLowerTriangular" | custom-call | tf_op jit(solution)/shard_map/jit(cholesky)/cholesky | solution.py:146
  239.7 11.7 %cholesky.215 = f32[128,128]{1,0:T(8,128)S(1)} custom-call(f32[128,128]{1,0:T(8,128)S(1)} %cholesky.267), custom_call_target="Cholesky" | custom-call | tf_op jit(solution)/shard_map/jit(cholesky)/cholesky | solution.py:146
  252.8 10.0 %custom-call.33 = f32[1,128,128]{1,2,0:T(8,128)S(1)} custom-call(f32[1,128,128]{2,1,0:T(8,128)S(1)} %get-tuple-element.72), custom_call_target="InvertDiagBlocksLowerTriangular" | custom-call | tf_op jit(solution)/shard_map/jit(cholesky)/cholesky | solution.py:146
  263.4 11.7 %cholesky.236 = f32[128,128]{1,0:T(8,128)S(1)} custom-call(f32[128,128]{1,0:T(8,128)S(1)} %cholesky.272), custom_call_target="Cholesky" | custom-call | tf_op jit(solution)/shard_map/jit(cholesky)/cholesky | solution.py:146
  275.9 9.8 %custom-call.34 = f32[1,128,128]{1,2,0:T(8,128)S(1)} custom-call(f32[1,128,128]{2,1,0:T(8,128)S(1)} %get-tuple-element.69), custom_call_target="InvertDiagBlocksLowerTriangular" | custom-call | tf_op jit(solution)/shard_map/jit(cholesky)/cholesky | solution.py:146
  286.3 12.0 %cholesky.253 = f32[128,128]{1,0:T(8,128)S(1)} custom-call(f32[128,128]{1,0:T(8,128)S(1)} %convolution_subtract_fusion.2), custom_call_target="Cholesky" | custom-call | tf_op jit(solution)/shard_map/jit(cholesky)/cholesky | solution.py:146
  301.6 10.1 %while.1 = (s32[]{:T(128)}, f32[512,512]{1,0:T(8,128)S(1)}, s32[4,2]{0,1:T(2,128)S(1)}, f32[4,128,128]{2,1,0:T(8,128)}, s32[]{:T(128)}) while((s32[]{:T(128)}, f32[512,512]{1,0:T(8,128)S(1)}, s32[4,2]{0,1:T(2,128)S(1)}, f32[4,128,128]{2,1,0:T(8,128)}, s32[]{:T(128)}) %tuple.51), condition=%wide.while_cond, body=%wide.while_body.sunk | while | flops 2 | bytes 132705 | solution.py:148
  311.7 40.1 %custom-call.35 = f32[4,128,128]{1,2,0:T(8,128)S(1)} custom-call(f32[4,128,128]{2,1,0:T(8,128)} %get-tuple-element.12), custom_call_target="InvertDiagBlocksLowerTriangular" | custom-call | tf_op jit(solution)/shard_map/triangular_solve | solution.py:148
  (159 shorter events, 68.6 us)
Async XLA Ops:
  3.3 5.8 %copy-start.6 = (s32[64]{0:T(128)S(1)}, s32[64]{0:T(128)}, u32[]{:S(2)}) copy-start(s32[64]{0:T(128)} %param.13) | copy-start | bytes 772
  3.3 5.8 %copy-start.7 = (f32[64]{0:T(128)S(1)}, f32[64]{0:T(128)}, u32[]{:S(2)}) copy-start(f32[64]{0:T(128)} %param.14) | copy-start | bytes 772
  4.6 6.8 %collective-permute-start = (f32[3,2,2,128,128]{4,3,2,1,0:T(8,128)}, f32[3,2,2,128,128]{4,3,2,1,0:T(8,128)}, u32[]{:S(2)}, u32[]{:S(2)}) collective-permute-start(f32[3,2,2,128,128]{4,3,2,1,0:T(8,128)} %get-tuple-element.40), channel_id=1, source_target_pairs={{0,1},{1,2},{2,3},{3,4},{4,5},{5,6},{6,7},{8,9},{9,10},{10,11},{11... | collective-permute-start | bytes 2359304 | tf_op jit(solution)/shard_map/ppermute | solution.py:24
  7.8 5.8 %collective-permute-start.1 = (f32[3,2,2,128,128]{4,3,2,1,0:T(8,128)}, f32[3,2,2,128,128]{4,3,2,1,0:T(8,128)}, u32[]{:S(2)}, u32[]{:S(2)}) collective-permute-start(f32[3,2,2,128,128]{4,3,2,1,0:T(8,128)} %get-tuple-element.41), channel_id=1, source_target_pairs={{1,0},{2,1},{3,2},{4,3},{5,4},{6,5},{7,6},{9,8},{10,9},{11,10},{12... | collective-permute-start | bytes 2359304 | tf_op jit(solution)/shard_map/ppermute | solution.py:26
  22.8 13.0 %collective-permute-start.2 = (f32[2,2,2,128,128]{4,3,2,1,0:T(8,128)S(1)}, f32[2,2,2,128,128]{4,3,2,1,0:T(8,128)S(1)}, u32[]{:S(2)}, u32[]{:S(2)}) collective-permute-start(f32[2,2,2,128,128]{4,3,2,1,0:T(8,128)S(1)} %get-tuple-element.60), channel_id=1, source_target_pairs={{0,1},{1,2},{2,3},{3,4},{4,5},{5,6},{6,7},{8,9},{9,10},{10,11},{11... | collective-permute-start | bytes 1572872 | tf_op jit(solution)/shard_map/ppermute | solution.py:24
  34.3 3.8 %collective-permute-start.3 = (f32[2,2,2,128,128]{4,3,2,1,0:T(8,128)S(1)}, f32[2,2,2,128,128]{4,3,2,1,0:T(8,128)S(1)}, u32[]{:S(2)}, u32[]{:S(2)}) collective-permute-start(f32[2,2,2,128,128]{4,3,2,1,0:T(8,128)S(1)} %get-tuple-element.61), channel_id=1, source_target_pairs={{1,0},{2,1},{3,2},{4,3},{5,4},{6,5},{7,6},{9,8},{10,9},{11,10},{12... | collective-permute-start | bytes 1572872 | tf_op jit(solution)/shard_map/ppermute | solution.py:26
  45.8 10.1 %collective-permute-start.4 = (f32[2,2,2,128,128]{4,3,2,1,0:T(8,128)S(1)}, f32[2,2,2,128,128]{4,3,2,1,0:T(8,128)S(1)}, u32[]{:S(2)}, u32[]{:S(2)}) collective-permute-start(f32[2,2,2,128,128]{4,3,2,1,0:T(8,128)S(1)} %get-tuple-element.56), channel_id=1, source_target_pairs={{0,1},{1,2},{2,3},{3,4},{4,5},{5,6},{6,7},{8,9},{9,10},{10,11},{11... | collective-permute-start | bytes 1572872 | tf_op jit(solution)/shard_map/ppermute | solution.py:24
  54.5 3.8 %collective-permute-start.5 = (f32[2,2,2,128,128]{4,3,2,1,0:T(8,128)S(1)}, f32[2,2,2,128,128]{4,3,2,1,0:T(8,128)S(1)}, u32[]{:S(2)}, u32[]{:S(2)}) collective-permute-start(f32[2,2,2,128,128]{4,3,2,1,0:T(8,128)S(1)} %get-tuple-element.57), channel_id=1, source_target_pairs={{1,0},{2,1},{3,2},{4,3},{5,4},{6,5},{7,6},{9,8},{10,9},{11,10},{12... | collective-permute-start | bytes 1572872 | tf_op jit(solution)/shard_map/ppermute | solution.py:26
  65.9 10.1 %collective-permute-start.6 = (f32[2,2,2,128,128]{4,3,2,1,0:T(8,128)S(1)}, f32[2,2,2,128,128]{4,3,2,1,0:T(8,128)S(1)}, u32[]{:S(2)}, u32[]{:S(2)}) collective-permute-start(f32[2,2,2,128,128]{4,3,2,1,0:T(8,128)S(1)} %get-tuple-element.52), channel_id=1, source_target_pairs={{0,1},{1,2},{2,3},{3,4},{4,5},{5,6},{6,7},{8,9},{9,10},{10,11},{11... | collective-permute-start | bytes 1572872 | tf_op jit(solution)/shard_map/ppermute | solution.py:24
  74.7 3.8 %collective-permute-start.7 = (f32[2,2,2,128,128]{4,3,2,1,0:T(8,128)S(1)}, f32[2,2,2,128,128]{4,3,2,1,0:T(8,128)S(1)}, u32[]{:S(2)}, u32[]{:S(2)}) collective-permute-start(f32[2,2,2,128,128]{4,3,2,1,0:T(8,128)S(1)} %get-tuple-element.53), channel_id=1, source_target_pairs={{1,0},{2,1},{3,2},{4,3},{5,4},{6,5},{7,6},{9,8},{10,9},{11,10},{12... | collective-permute-start | bytes 1572872 | tf_op jit(solution)/shard_map/ppermute | solution.py:26
  86.1 11.8 %copy-start = (f32[2,4,128,128]{3,2,1,0:T(8,128)S(1)}, f32[2,4,128,128]{3,2,1,0:T(8,128)}, u32[]{:S(2)}) copy-start(f32[2,4,128,128]{3,2,1,0:T(8,128)} %param.10) | copy-start | bytes 1572868
  86.1 17.3 %copy-start.2 = (s32[512,8]{0,1:T(8,128)S(1)}, s32[512,8]{0,1:T(8,128)}, u32[]{:S(2)}) copy-start(s32[512,8]{0,1:T(8,128)} %param.15) | copy-start | bytes 49156
  86.1 17.8 %copy-start.4 = (f32[512,8]{0,1:T(8,128)S(1)}, f32[512,8]{0,1:T(8,128)}, u32[]{:S(2)}) copy-start(f32[512,8]{0,1:T(8,128)} %param.16) | copy-start | bytes 49156
  87.2 16.9 %collective-permute-start.8 = (f32[2,2,2,128,128]{4,3,2,1,0:T(8,128)}, f32[2,2,2,128,128]{4,3,2,1,0:T(8,128)}, u32[]{:S(2)}, u32[]{:S(2)}) collective-permute-start(f32[2,2,2,128,128]{4,3,2,1,0:T(8,128)} %get-tuple-element.48), channel_id=1, source_target_pairs={{0,1},{1,2},{2,3},{3,4},{4,5},{5,6},{6,7},{8,9},{9,10},{10,11},{11... | collective-permute-start | bytes 1572872 | tf_op jit(solution)/shard_map/ppermute | solution.py:24
  96.6 7.5 %collective-permute-start.9 = (f32[2,2,2,128,128]{4,3,2,1,0:T(8,128)}, f32[2,2,2,128,128]{4,3,2,1,0:T(8,128)}, u32[]{:S(2)}, u32[]{:S(2)}) collective-permute-start(f32[2,2,2,128,128]{4,3,2,1,0:T(8,128)} %get-tuple-element.49), channel_id=1, source_target_pairs={{1,0},{2,1},{3,2},{4,3},{5,4},{6,5},{7,6},{9,8},{10,9},{11,10},{12... | collective-permute-start | bytes 1572872 | tf_op jit(solution)/shard_map/ppermute | solution.py:26
  99.0 21.9 %all-to-all-start = ((f32[2,4,128,128]{3,1,0,2:T(4,128)}), f32[2,4,128,128]{3,1,0,2:T(4,128)}, u32[]{:S(2)}, u32[]{:S(2)}) async-start(f32[2,4,128,128]{3,1,0,2:T(4,128)} %copy.32), calls=%async_computation | async-start | bytes 1048576 | tf_op jit(solution)/shard_map/all_to_all | solution.py:153
  112.8 8.1 %copy-start.3 = (f32[512]{0:T(512)S(1)}, f32[512]{0:T(512)}, u32[]{:S(2)}) copy-start(f32[512]{0:T(512)} %param.18) | copy-start | bytes 6148
  113.9 9.1 %collective-permute-start.10 = (f32[2,2,2,128,128]{4,3,2,1,0:T(8,128)}, f32[2,2,2,128,128]{4,3,2,1,0:T(8,128)}, u32[]{:S(2)}, u32[]{:S(2)}) collective-permute-start(f32[2,2,2,128,128]{4,3,2,1,0:T(8,128)} %get-tuple-element.44), channel_id=1, source_target_pairs={{0,1},{1,2},{2,3},{3,4},{4,5},{5,6},{6,7},{8,9},{9,10},{10,11},{11... | collective-permute-start | bytes 1572872 | tf_op jit(solution)/shard_map/ppermute | solution.py:24
  119.1 4.1 %collective-permute-start.11 = (f32[2,2,2,128,128]{4,3,2,1,0:T(8,128)}, f32[2,2,2,128,128]{4,3,2,1,0:T(8,128)}, u32[]{:S(2)}, u32[]{:S(2)}) collective-permute-start(f32[2,2,2,128,128]{4,3,2,1,0:T(8,128)} %get-tuple-element.45), channel_id=1, source_target_pairs={{1,0},{2,1},{3,2},{4,3},{5,4},{6,5},{7,6},{9,8},{10,9},{11,10},{12... | collective-permute-start | bytes 1572872 | tf_op jit(solution)/shard_map/ppermute | solution.py:26
  263.4 88.4 %copy-start.5 = (f32[8,512]{1,0:T(8,128)S(1)}, f32[8,512]{1,0:T(8,128)}, u32[]{:S(2)}) copy-start(f32[8,512]{1,0:T(8,128)} %param.19) | copy-start | bytes 49156
  263.4 88.4 %copy-start.8 = (f32[512]{0:T(512)S(1)}, f32[512]{0:T(512)}, u32[]{:S(2)}) copy-start(f32[512]{0:T(512)} %param.17) | copy-start | bytes 6148
  301.4 53.6 %copy-start.1 = (f32[2,4,4,32,128]{4,0,2,3,1:T(2,128)S(1)}, f32[2,4,4,32,128]{4,0,2,3,1:T(2,128)}, u32[]{:S(2)}) copy-start(f32[2,4,4,32,128]{4,0,2,3,1:T(2,128)} %copy.33) | copy-start | bytes 1572868
where the time goes:
time: 364 us; the launch traced here: 357 us
  other arithmetic  175 us (48%)
  starting transfers between devices  59.6 us (16%)
  local copies, waits for them, and re-layouts  59.1 us (16%)
  blocking collectives  43.1 us (12%)
  waiting for transfers between devices  9.83 us (3%)
  matrix products  6.62 us (2%)
  between operations  3.9 us (1%)
    another operation x15, other arithmetic, body(): factor = jnp.linalg.cholesky(cov)  79.5 us
    ppermute x6, starting transfers between devices, padded(): lax.ppermute(tail, axis, [(i, (i + 1) % count) for i in range(ends)])  46.8 us
    another operation x3, other arithmetic, body(): lax.linalg.triangular_solve(factor, half, left_side=True, lower=True, tra...  40.3 us
    psum x1, blocking collectives, body(): summed = lax.psum(partial_value, 'space')  34.5 us
    mul x6, other arithmetic, body(): saturate(perm_pad, pad_plane(sat_ext), pad_plane(press_ext), source_wide)  21.3 us
    gather x1, local copies, waits for them, and re-layouts, body(): picked = jnp.take(flat, jnp.where(valid, local, 0), axis=1)  21.3 us
    div x1, local copies, waits for them, and re-layouts, pressure(): return numer / denom  16.4 us
    mul x12, other arithmetic, props(): return (perm * total, water / total)  13.8 us
  transfers between devices with their start and end apart: 13, of which 6 were waited for; matrix products, arithmetic and copies ran while one was open for 4% of the time, Pallas kernels for 0%

commit v1 on v0

v1 whole, which is shorter than its diff:
```python
import functools

import jax
import jax.numpy as jnp
from jax import lax
from jax.experimental import pallas as pl
from jax.experimental.pallas import tpu as pltpu
from jax.sharding import PartitionSpec as P

SWEEPS = 6
time_step = 0.1
inflation = 4.0

MESH = pl.DeviceIdType.MESH
HIGH = lax.Precision.HIGHEST
SUB = 8
LANES = 128
CHUNK = 4


def iota(shape, dim):
    return lax.broadcasted_iota(jnp.int32, shape, dim)


def as_float(cond):
    return jnp.where(cond, 1.0, 0.0).astype(jnp.float32)


def kernel(
    n_mem,
    n_space,
    lp,
    sat,
    pre,
    wells,
    rate,
    oi,
    ow,
    ov,
    var,
    noise,
    out,
    S,
    L,
    F,
    Q,
    half_perm,
    src,
    lp_ghost,
    sat_ghost,
    pre_ghost,
    cols,
    pred,
    gram,
    first_send,
    first_recv,
    s_send,
    s_recv,
    p_send,
    p_recv,
    col_send,
    col_recv,
    pred_send,
    pred_recv,
    gram_send,
    gram_recv,
):
    members, width, ny, nz = lp.shape
    yl = ny // SUB
    part = ny // n_mem
    ens = members * n_mem
    total_rows = width * n_space
    nobs = oi.shape[1]
    taps = oi.shape[0]
    per_row = nobs // total_rows
    row_taps = taps * per_row
    local_obs = per_row * width
    plane = ny * nz
    mem = lax.axis_index("mem")
    place = lax.axis_index("space")
    has_left = place > 0
    has_right = place < n_space - 1

    barrier = pltpu.get_barrier_semaphore()
    for d in range(1, n_mem):
        pl.semaphore_signal(
            barrier, inc=1, device_id=(lax.rem(mem + d, n_mem), place), device_id_type=MESH
        )
    for d in range(1, n_space):
        pl.semaphore_signal(
            barrier, inc=1, device_id=(mem, lax.rem(place + d, n_space)), device_id_type=MESH
        )

    def clear(row, side):
        S[:, :, row] = jnp.zeros_like(S[:, :, row])
        Q[:, :, row] = jnp.zeros_like(Q[:, :, row])
        lp_ghost[side] = jnp.zeros_like(lp_ghost[side])
        sat_ghost[side] = jnp.zeros_like(sat_ghost[side])
        pre_ghost[side] = jnp.zeros_like(pre_ghost[side])

    @pl.when(jnp.logical_not(has_left))
    def _():
        clear(0, 0)

    @pl.when(jnp.logical_not(has_right))
    def _():
        clear(width + 1, 1)

    pl.semaphore_wait(barrier, n_mem - 1 + n_space - 1)

    def remote(a, b, send, recv, target):
        return pltpu.make_async_remote_copy(
            src_ref=a, dst_ref=b, send_sem=send, recv_sem=recv, device_id=target, device_id_type=MESH
        )

    right = (mem, lax.rem(place + 1, n_space))
    left = (mem, lax.rem(place + n_space - 1, n_space))

    def first(side):
        row = width - 1 if side == 0 else 0
        target = right if side == 0 else left
        pairs = [
            (pre.at[row], pre_ghost.at[side]),
            (sat.at[row], sat_ghost.at[side]),
            (lp.at[:, row], lp_ghost.at[side]),
        ]
        return [
            remote(a, b, first_send.at[side, i], first_recv.at[side, i], target)
            for i, (a, b) in enumerate(pairs)
        ]

    def halo(field, send, recv, k, m, side):
        a = width if side == 0 else 1
        b = 0 if side == 0 else width + 1
        rows = pl.ds(1, yl)
        return remote(
            field.at[k, m, a, rows],
            field.at[k, m, b, rows],
            send.at[k, m, side],
            recv.at[k, m, side],
            right if side == 0 else left,
        )

    def each(make, to_do, sending):
        for side in (0, 1):
            there = (has_right, has_left)[side if sending else 1 - side]

            @pl.when(there)
            def _(side=side):
                for copy in make(side):
                    getattr(copy, to_do)()

    each(first, "start", True)

    def column(d):
        peer = lax.rem(mem + d, n_mem)
        return remote(
            lp.at[:, :, pl.ds(pl.multiple_of(peer * part, part), part)],
            cols.at[pl.ds(mem * members, members)],
            col_send.at[d],
            col_recv.at[d],
            (peer, place),
        )

    for d in range(1, n_mem):
        column(d).start()
    for m in range(members):
        cols[mem * members + m] = lp[m, :, pl.ds(pl.multiple_of(mem * part, part), part)]

    def strided(ref, lead, c):
        return ref[(*lead, pl.ds(c, SUB, stride=yl), slice(None))]

    def props(half, s):
        water = s * s
        dry = 1.0 - s
        total = water + dry * dry * 0.25
        return half * total, water / total

    sub = iota((SUB, nz), 0)
    lane = iota((SUB, nz), 1)
    inner = as_float(lane < nz - 1)
    not_first = as_float(lane > 0)
    ends = as_float((lane == 0) | (lane == nz - 1))
    sub_first = sub == 0
    sub_last = sub == SUB - 1

    def pads(field, k, m, r):
        top = field[k, m, r, yl]
        field[k, m, r, 0] = jnp.where(sub_first, 0.0, pltpu.roll(top, 1, 0))
        bottom = field[k, m, r, 1]
        field[k, m, r, yl + 1] = jnp.where(sub_last, 0.0, pltpu.roll(bottom, SUB - 1, 0))

    def load_row(m, r):
        for c in range(yl):
            half = 0.5 * jnp.exp(strided(lp, (m, r), c))
            s = strided(sat, (r,), c)
            lam, frac = props(half, s)
            half_perm[m, r + 1, c] = half
            S[0, m, r + 1, c + 1] = s
            L[0, m, r + 1, c + 1] = lam
            F[0, m, r + 1, c + 1] = frac
            Q[0, m, r + 1, c + 1] = strided(pre, (r,), c)
        pads(L, 0, m, r + 1)
        pads(F, 0, m, r + 1)
        pads(Q, 0, m, r + 1)

    for m in range(members):

        @pl.loop(0, width)
        def _(r, m=m):
            load_row(m, r)

    well = wells[...].astype(jnp.float32)
    well_x = jnp.floor((well + 0.5) * (1.0 / plane))
    rest = well - well_x * plane
    well_y = jnp.floor((rest + 0.5) * (1.0 / nz))
    well_z = rest - well_y * nz
    count = well.shape[1]
    pos = iota((ny, count), 0)
    held_y = ((pos % SUB) * yl + pos // SUB).astype(jnp.float32)
    at_z = as_float(pos.astype(jnp.float32) == well_z)
    at_y = held_y == well_y
    for r in range(width):
        here = well_x == (place * width + r).astype(jnp.float32)
        at_row = jnp.where(at_y & here, rate[...], 0.0)
        field = lax.dot_general(
            at_row, at_z, (((1,), (1,)), ((), ())), precision=HIGH, preferred_element_type=jnp.float32
        )
        src[r] = field.reshape(yl, SUB, nz)

    def dot(a, b):
        return jnp.dot(a, b, precision=HIGH, preferred_element_type=jnp.float32)

    index_all = oi[...].astype(jnp.float32)
    weight_all = ow[...]
    from_obs = iota((nobs, row_taps), 0)
    tap_lane = iota((nobs, row_taps), 1)
    own_tap = iota((taps, row_taps), 0) == iota((taps, row_taps), 1) // per_row
    tap_pos = iota((ny, row_taps), 0)
    tap_y = ((tap_pos % SUB) * yl + tap_pos // SUB).astype(jnp.float32)
    tap_z = tap_pos.astype(jnp.float32)
    z_hot, y_hot, gather_taps = [], [], []
    for r in range(width):
        x = place * width + r
        select = as_float(from_obs == x + total_rows * (tap_lane % per_row))
        index = jnp.sum(jnp.where(own_tap, dot(index_all, select), 0.0), axis=0, keepdims=True)
        weight = jnp.sum(jnp.where(own_tap, dot(weight_all, select), 0.0), axis=0, keepdims=True)
        rest = index - (x * plane).astype(jnp.float32)
        cell_y = jnp.floor((rest + 0.5) * (1.0 / nz))
        cell_z = rest - cell_y * nz
        z_hot.append(as_float(tap_z == cell_z))
        y_hot.append(jnp.where(tap_y == cell_y, weight, 0.0))
        gather_taps.append(
            as_float(
                iota((row_taps, LANES), 1) == r * per_row + iota((row_taps, LANES), 0) % per_row
            )
        )
    obs_lane = iota((nobs, LANES), 1)
    own_obs = as_float(
        (iota((nobs, LANES), 0) == place * width + obs_lane // per_row + total_rows * (obs_lane % per_row))
        & (obs_lane < local_obs)
    )
    noise_own = dot(noise[...], own_obs)
    value_own = dot(jnp.broadcast_to(ov[...], (SUB, nobs)), own_obs)
    var_own = dot(jnp.broadcast_to(var[...], (SUB, nobs)), own_obs)

    each(first, "wait_recv", False)
    for side in (0, 1):
        row = 0 if side == 0 else width + 1
        there = as_float(has_left if side == 0 else has_right)
        for c in range(yl):
            s = strided(sat_ghost, (side,), c)
            p = strided(pre_ghost, (side,), c)
            for m in range(members):
                half = 0.5 * there * jnp.exp(strided(lp_ghost, (side, m), c))
                lam, frac = props(half, s)
                half_perm[m, row, c] = half
                L[0, m, row, c + 1] = lam
                F[0, m, row, c + 1] = frac
                Q[0, m, row, c + 1] = p

    def beside(field, k, m, r, c):
        mid = pl.ds(1 + c, CHUNK)
        return [
            field[k, m, r + 1, mid],
            field[k, m, r - 1, mid],
            field[k, m, r, pl.ds(c + 2, CHUNK)],
            field[k, m, r, pl.ds(c, CHUNK)],
        ]

    def saturate(k, m, r):
        for c in range(0, yl, CHUNK):
            mid = pl.ds(1 + c, CHUNK)
            lam, frac, press = L[k, m, r, mid], F[k, m, r, mid], Q[k, m, r, mid]
            lam_next = pltpu.roll(lam, nz - 1, 2)
            frac_next = pltpu.roll(frac, nz - 1, 2)
            press_next = pltpu.roll(press, nz - 1, 2)
            flux = (lam + lam_next) * inner * (press - press_next)
            along = flux * jnp.where(flux > 0.0, frac, frac_next)
            outflow = along - pltpu.roll(along, 1, 2)
            outflow = outflow + ends * jnp.maximum(lam * press, 0.0) * frac
            for lam_j, frac_j, press_j in zip(
                beside(L, k, m, r, c), beside(F, k, m, r, c), beside(Q, k, m, r, c)
            ):
                flux = (lam + lam_j) * (press - press_j)
                outflow = outflow + flux * jnp.where(flux > 0.0, frac, frac_j)
            source = src[r - 1, pl.ds(c, CHUNK)]
            water = jnp.maximum(source, 0.0) + jnp.minimum(source, 0.0) * frac
            s = jnp.clip(S[k, m, r, mid] + time_step * (water - outflow), 0.0, 1.0)
            lam, frac = props(half_perm[m, r, pl.ds(c, CHUNK)], s)
            S[k + 1, m, r, mid] = s
            L[k + 1, m, r, mid] = lam
            F[k + 1, m, r, mid] = frac
        pads(L, k + 1, m, r)
        pads(F, k + 1, m, r)

    def pressure(k, m, r):
        for c in range(0, yl, CHUNK):
            mid = pl.ds(1 + c, CHUNK)
            lam, press = L[k + 1, m, r, mid], Q[k, m, r, mid]
            lam_j = beside(L, k + 1, m, r, c) + [
                pltpu.roll(lam, 1, 2) * not_first,
                pltpu.roll(lam, nz - 1, 2) * inner,
            ]
            press_j = beside(Q, k, m, r, c) + [
                pltpu.roll(press, 1, 2) * not_first,
                pltpu.roll(press, nz - 1, 2) * inner,
            ]
            denom = 1.0 + 6.0 * lam + sum(lam_j[1:], lam_j[0])
            numer = press + src[r - 1, pl.ds(c, CHUNK)] + lam * sum(press_j[1:], press_j[0])
            for a, b in zip(lam_j, press_j):
                numer = numer + a * b
            Q[k + 1, m, r, mid] = numer / denom
        pads(Q, k + 1, m, r)

    def ghost_props(k, m, row):
        for c in range(0, yl, CHUNK):
            mid = pl.ds(1 + c, CHUNK)
            lam, frac = props(half_perm[m, row, pl.ds(c, CHUNK)], S[k, m, row, mid])
            L[k, m, row, mid] = lam
            F[k, m, row, mid] = frac

    def s_halo(k, m):
        return lambda side: [halo(S, s_send, s_recv, k, m, side)]

    def p_halo(k, m):
        return lambda side: [halo(Q, p_send, p_recv, k, m, side)]

    def inside(step, k, m):
        @pl.loop(2, width)
        def _(r):
            step(k, m, r)

    def border(step, k, m):
        @pl.loop(0, 2)
        def _(i):
            step(k, m, 1 + i * (width - 1))

    @pl.loop(0, SWEEPS)
    def _(k):
        for m in range(members):
            inside(saturate, k, m)
        for m in range(members):

            @pl.when(k > 0)
            def _(m=m):
                each(p_halo(k, m), "wait_recv", False)

            border(saturate, k, m)
            each(s_halo(k + 1, m), "start", True)
        for m in range(members):
            inside(pressure, k, m)
        for m in range(members):
            each(s_halo(k + 1, m), "wait_recv", False)

            @pl.loop(0, 2)
            def _(i, m=m):
                ghost_props(k + 1, m, i * (width + 1))

            border(pressure, k, m)

            @pl.when(k + 1 < SWEEPS)
            def _(m=m):
                each(p_halo(k + 1, m), "start", True)

    member_row = iota((ens, LANES), 0)
    own = jnp.zeros((ens, LANES), jnp.float32)
    for r in range(width):
        found = jnp.zeros((ens, row_taps), jnp.float32)
        for m in range(members):
            field = Q[SWEEPS, m, r + 1, pl.ds(1, yl)].reshape(ny, nz)
            picked = jnp.sum(dot(field, z_hot[r]) * y_hot[r], axis=0, keepdims=True)
            found = jnp.where(iota((ens, row_taps), 0) == mem * members + m, picked, found)
        own = own + dot(found, gather_taps[r])
    pred[mem] = own

    def share(d):
        return remote(
            pred.at[mem], pred.at[mem], pred_send.at[d], pred_recv.at[d], (lax.rem(mem + d, n_mem), place)
        )

    for d in range(1, n_mem):
        share(d).start()
    scale = jnp.where(iota((ens, LANES), 1) < local_obs, inflation * var_own, 1.0)
    inverse = jnp.where(iota((ens, LANES), 1) < local_obs, 1.0 / scale, 0.0)
    target_obs = value_own + jnp.sqrt(inflation * var_own) * noise_own
    for d in range(1, n_mem):
        share(d).wait_recv()
    predicted = pred[0]
    for a in range(1, n_mem):
        predicted = predicted + pred[a]
    dev = predicted - jnp.mean(predicted, axis=0, keepdims=True)
    resid = target_obs - predicted
    both = jnp.concatenate([dev, resid, jnp.zeros((LANES - 2 * ens, LANES), jnp.float32)], axis=0)
    gram[place] = lax.dot_general(
        dev * inverse, both, (((1,), (1,)), ((), ())), precision=HIGH, preferred_element_type=jnp.float32
    )

    def sum_part(d):
        return remote(
            gram.at[place],
            gram.at[place],
            gram_send.at[d],
            gram_recv.at[d],
            (mem, lax.rem(place + d, n_space)),
        )

    for d in range(1, n_space):
        sum_part(d).start()
    for d in range(1, n_mem):
        column(d).wait_recv()
    for d in range(1, n_space):
        sum_part(d).wait_recv()
    whole = gram[0]
    for a in range(1, n_space):
        whole = whole + gram[a]

    row_id = iota((ens, LANES), 0)
    lane_id = iota((ens, LANES), 1)
    table = whole / (ens - 1) + as_float(row_id == lane_id)
    for i in range(ens):
        pivot_row = table[i : i + 1, :] / table[i : i + 1, i : i + 1]
        table = jnp.where(row_id == i, pivot_row, table - table[:, i : i + 1] * pivot_row)
    mixing = (
        table - jnp.mean(table, axis=0, keepdims=True) + as_float(row_id + ens == lane_id)
    )
    for m in range(ens):
        factors = [
            jnp.broadcast_to(mixing[j : j + 1, ens + m : ens + m + 1], (SUB, nz)) for j in range(ens)
        ]
        for r in range(width):
            for c in range(0, part, SUB):
                total = factors[0] * cols[0, r, pl.ds(c, SUB)]
                for j in range(1, ens):
                    total = total + factors[j] * cols[j, r, pl.ds(c, SUB)]
                out[m, r, pl.ds(c, SUB)] = total

    each(first, "wait_send", True)
    for d in range(1, n_mem):
        column(d).wait_send()
        share(d).wait_send()
    for d in range(1, n_space):
        sum_part(d).wait_send()

    @pl.loop(1, SWEEPS + 1)
    def _(k):
        for m in range(members):
            each(s_halo(k, m), "wait_send", True)

            @pl.when(k < SWEEPS)
            def _(m=m):
                each(p_halo(k, m), "wait_send", True)


def body(
    log_perm,
    saturation,
    pressure_init,
    wells,
    well_rate,
    obs_index,
    obs_weight,
    obs_value,
    obs_var,
    noise,
):
    n_mem = lax.axis_size("mem")
    n_space = lax.axis_size("space")
    members, width, ny, nz = log_perm.shape
    ens = members * n_mem
    yl = ny // SUB
    part = ny // n_mem
    vmem = pl.BlockSpec(memory_space=pltpu.VMEM)
    state = pltpu.VMEM((SWEEPS + 1, members, width + 2, yl + 2, SUB, nz), jnp.float32)
    dma = pltpu.SemaphoreType.DMA
    return pl.pallas_call(
        functools.partial(kernel, n_mem, n_space),
        out_shape=jax.ShapeDtypeStruct((ens, width, part, nz), jnp.float32),
        in_specs=[vmem] * 10,
        out_specs=vmem,
        scratch_shapes=[
            state,
            state,
            state,
            state,
            pltpu.VMEM((members, width + 2, yl, SUB, nz), jnp.float32),
            pltpu.VMEM((width, yl, SUB, nz), jnp.float32),
            pltpu.VMEM((2, members, ny, nz), jnp.float32),
            pltpu.VMEM((2, ny, nz), jnp.float32),
            pltpu.VMEM((2, ny, nz), jnp.float32),
            pltpu.VMEM((ens, width, part, nz), jnp.float32),
            pltpu.VMEM((n_mem, ens, LANES), jnp.float32),
            pltpu.VMEM((n_space, ens, LANES), jnp.float32),
            dma((2, 3)),
            dma((2, 3)),
            dma((SWEEPS + 1, members, 2)),
            dma((SWEEPS + 1, members, 2)),
            dma((SWEEPS + 1, members, 2)),
            dma((SWEEPS + 1, members, 2)),
            dma((n_mem,)),
            dma((n_mem,)),
            dma((n_mem,)),
            dma((n_mem,)),
            dma((n_space,)),
            dma((n_space,)),
        ],
        compiler_params=pltpu.CompilerParams(
            collective_id=0, has_side_effects=True, vmem_limit_bytes=48 * 1024 * 1024
        ),
    )(
        log_perm,
        saturation,
        pressure_init,
        wells[None],
        well_rate[None],
        obs_index.T,
        obs_weight.T,
        obs_value[None],
        obs_var[None],
        noise,
    )


def solution(mesh):
    placed = (
        P("mem", "space", None, None),
        P("space", None, None),
        P("space", None, None),
        P(),
        P(),
        P(),
        P(),
        P(),
        P(),
        P(),
    )
    return jax.shard_map(
        body, mesh=mesh, in_specs=placed, out_specs=P(None, "space", "mem", None), check_vma=False
    )
```

time: 364 us -> 66.5 us (0.18); the launches traced: 357 us -> 66.1 us
  other arithmetic: 175 us -> 0 us
  starting transfers between devices: 59.6 us -> 0 us
  Pallas kernels: 0 us -> 59.5 us
  local copies, waits for them, and re-layouts: 59.1 us -> 6.59 us
  blocking collectives: 43.1 us -> 0 us
  waiting for transfers between devices: 9.83 us -> 0 us
  matrix products: 6.62 us -> 0 us
  between operations: 3.9 us -> 0.02 us
    another operation x29 -> x0, other arithmetic: 128 us -> none  [the longest x15 79.5 us: body(): factor = jnp.linalg.cholesky(cov)]
    pallas_call x0 -> x1, Pallas kernels: none -> 59.5 us  [body(): pl.pallas_call(functools.partial(kernel, n_mem, n_space), out_shape=jax.S...]
    ppermute x12 -> x0, starting transfers between devices: 55.2 us -> none  [the longest x6 46.8 us: padded(): lax.ppermute(tail, axis, [(i, (i + 1) % count) for i in range(ends)])]
    mul x18 -> x0, other arithmetic: 35.1 us -> none  [the longest x6 21.3 us: body(): saturate(perm_pad, pad_plane(sat_ext), pad_plane(press_ext), source_wide)]
    psum x1 -> x0, blocking collectives: 34.5 us -> none  [body(): summed = lax.psum(partial_value, 'space')]
    gather x1 -> x0, local copies, waits for them, and re-layouts: 21.3 us -> none  [body(): picked = jnp.take(flat, jnp.where(valid, local, 0), axis=1)]
    div x2 -> x0, local copies, waits for them, and re-layouts: 16.7 us -> none  [the longest x1 16.4 us: pressure(): return numer / denom]
    another operation x24 -> x0, local copies, waits for them, and re-layouts: 13.5 us -> none
  transfers between devices with their start and end apart: 13 -> 0, of which waited for: 6 -> 0; matrix products, arithmetic and copies ran while one was open for 4% -> 0% of each run, Pallas kernels for 0% -> 0%
where the time goes in v1:
time: 66.5 us; the launch traced here: 66.1 us
  Pallas kernels  59.5 us (89%)
  local copies, waits for them, and re-layouts  6.59 us (10%)
    pallas_call x1, Pallas kernels, body(): pl.pallas_call(functools.partial(kernel, n_mem, n_space), out_shape=jax.S...  59.5 us
    unnamed x21, local copies, waits for them, and re-layouts  6.59 us

profile of v1, /device:TPU:0, one launch (start us, length us, event | category | flops | bytes accessed | tf_op | source)
XLA Modules:
  0.0 66.1 jit_solution(17198359631952250294)
XLA Ops:
  0.0 0.0 copy-start.7
  0.0 0.0 copy-start.6
  0.0 0.0 copy-start.8
  0.0 0.0 copy-start.9
  0.0 0.7 %copy-done.7 = f32[512]{0:T(512)S(1)} copy-done((f32[512]{0:T(512)S(1)}, f32[512]{0:T(512)}, u32[]{:S(2)}) %copy-start.7) | copy-done | bytes 2072
  0.7 0.0 copy-done.6
  0.7 0.0 copy-done.8
  0.7 0.0 copy-done.9
  0.7 0.0 copy-start
  0.7 1.0 %copy-done = f32[2,4,128,128]{3,2,1,0:T(8,128)S(1)} copy-done((f32[2,4,128,128]{3,2,1,0:T(8,128)S(1)}, f32[2,4,128,128]{3,2,1,0:T(8,128)}, u32[]{:S(2)}) %copy-start) | copy-done | bytes 524312
  1.7 0.0 copy-start.1
  1.7 0.9 %copy-done.1 = f32[4,128,128]{2,1,0:T(8,128)S(1)} copy-done((f32[4,128,128]{2,1,0:T(8,128)S(1)}, f32[4,128,128]{2,1,0:T(8,128)}, u32[]{:S(2)}) %copy-start.1) | copy-done | bytes 262168
  2.7 0.0 copy-start.2
  2.7 0.9 %copy-done.2 = f32[4,128,128]{2,1,0:T(8,128)S(1)} copy-done((f32[4,128,128]{2,1,0:T(8,128)S(1)}, f32[4,128,128]{2,1,0:T(8,128)}, u32[]{:S(2)}) %copy-start.2) | copy-done | bytes 262168
  3.6 0.0 copy-start.3
  3.6 0.7 %copy-done.3 = s32[512,8]{0,1:T(8,128)S(1)} copy-done((s32[512,8]{0,1:T(8,128)S(1)}, s32[512,8]{0,1:T(8,128)}, u32[]{:S(2)}) %copy-start.3) | copy-done | bytes 16408
  4.4 0.0 copy-start.4
  4.4 0.7 %copy-done.4 = f32[512,8]{0,1:T(8,128)S(1)} copy-done((f32[512,8]{0,1:T(8,128)S(1)}, f32[512,8]{0,1:T(8,128)}, u32[]{:S(2)}) %copy-start.4) | copy-done | bytes 16408
  5.1 0.0 copy-start.5
  5.1 0.7 %copy-done.5 = f32[8,512]{1,0:T(8,128)S(1)} copy-done((f32[8,512]{1,0:T(8,128)S(1)}, f32[8,512]{1,0:T(8,128)}, u32[]{:S(2)}) %copy-start.5) | copy-done | bytes 16408
  5.8 59.5 %shard_map.100 = f32[8,4,32,128]{3,2,1,0:T(8,128)S(1)} custom-call(f32[2,4,128,128]{3,2,1,0:T(8,128)S(1)} %copy-done, f32[4,128,128]{2,1,0:T(8,128)S(1)} %copy-done.1, f32[4,128,128]{2,1,0:T(8,128)S(1)} %copy-done.2, s32[1,64]{1,0:T(1,128)S(1)} %bitcast.10, f32[1,64]{1,0:T(1,128)S(1)} %bitcast.11, s32[8,512]{1,0:T(8,128)S(1)} %bitcast.6, ...), custom_call_target="tpu_custom_call" | custom-call | tf_op jit(solution)/shard_map/pallas_call | solution.py:496
  65.3 0.8 %copy.12 = f32[8,4,32,128]{3,2,1,0:T(8,128)} copy(f32[8,4,32,128]{3,2,1,0:T(8,128)S(1)} %shard_map.100) | data formatting | bytes 1048576
Async XLA Ops:
  0.0 0.7 %copy-start.7 = (f32[512]{0:T(512)S(1)}, f32[512]{0:T(512)}, u32[]{:S(2)}) copy-start(f32[512]{0:T(512)} %param.18) | copy-start | bytes 6148
  0.0 0.7 %copy-start.6 = (f32[512]{0:T(512)S(1)}, f32[512]{0:T(512)}, u32[]{:S(2)}) copy-start(f32[512]{0:T(512)} %param.17) | copy-start | bytes 6148
  0.0 0.7 %copy-start.8 = (s32[64]{0:T(128)S(1)}, s32[64]{0:T(128)}, u32[]{:S(2)}) copy-start(s32[64]{0:T(128)} %param.13) | copy-start | bytes 772
  0.0 0.7 %copy-start.9 = (f32[64]{0:T(128)S(1)}, f32[64]{0:T(128)}, u32[]{:S(2)}) copy-start(f32[64]{0:T(128)} %param.14) | copy-start | bytes 772
  0.7 1.0 %copy-start = (f32[2,4,128,128]{3,2,1,0:T(8,128)S(1)}, f32[2,4,128,128]{3,2,1,0:T(8,128)}, u32[]{:S(2)}) copy-start(f32[2,4,128,128]{3,2,1,0:T(8,128)} %lp.1) | copy-start | bytes 1572868
  1.7 0.9 %copy-start.1 = (f32[4,128,128]{2,1,0:T(8,128)S(1)}, f32[4,128,128]{2,1,0:T(8,128)}, u32[]{:S(2)}) copy-start(f32[4,128,128]{2,1,0:T(8,128)} %sat.1) | copy-start | bytes 786436
  2.7 0.9 %copy-start.2 = (f32[4,128,128]{2,1,0:T(8,128)S(1)}, f32[4,128,128]{2,1,0:T(8,128)}, u32[]{:S(2)}) copy-start(f32[4,128,128]{2,1,0:T(8,128)} %pre.1) | copy-start | bytes 786436
  3.6 0.7 %copy-start.3 = (s32[512,8]{0,1:T(8,128)S(1)}, s32[512,8]{0,1:T(8,128)}, u32[]{:S(2)}) copy-start(s32[512,8]{0,1:T(8,128)} %param.15) | copy-start | bytes 49156
  4.4 0.7 %copy-start.4 = (f32[512,8]{0,1:T(8,128)S(1)}, f32[512,8]{0,1:T(8,128)}, u32[]{:S(2)}) copy-start(f32[512,8]{0,1:T(8,128)} %param.16) | copy-start | bytes 49156
  5.1 0.7 %copy-start.5 = (f32[8,512]{1,0:T(8,128)S(1)}, f32[8,512]{1,0:T(8,128)}, u32[]{:S(2)}) copy-start(f32[8,512]{1,0:T(8,128)} %noise.1) | copy-start | bytes 49156

commit v2 on v1

--- a/solution.py
+++ b/solution.py
@@ -16,6 +16,7 @@
 SUB = 8
 LANES = 128
 CHUNK = 4
+PARTS = 2
 
 
 def iota(shape, dim):
@@ -24,11 +25,32 @@
 
 def as_float(cond):
     return jnp.where(cond, 1.0, 0.0).astype(jnp.float32)
+
+
+def split_dot(a, hot):
+    rows = a.shape[0]
+    high = a.astype(jnp.bfloat16).astype(jnp.float32)
+    rest = a - high
+    middle = rest.astype(jnp.bfloat16).astype(jnp.float32)
+    terms = jnp.concatenate([high, middle, rest - middle], axis=0).astype(jnp.bfloat16)
+    got = jnp.dot(terms, hot.astype(jnp.bfloat16), preferred_element_type=jnp.float32)
+    return got[:rows] + got[rows : 2 * rows] + got[2 * rows :]
 
 
 def kernel(
     n_mem,
     n_space,
+    lp_in,
+    sat_in,
+    pre_in,
+    wells_in,
+    rate_in,
+    oi_in,
+    ow_in,
+    ov_in,
+    var_in,
+    noise_in,
+    out,
     lp,
     sat,
     pre,
@@ -39,7 +61,11 @@
     ov,
     var,
     noise,
-    out,
+    z_hot,
+    y_hot,
+    tap_sum,
+    obs_own,
+    local_sem,
     S,
     L,
     F,
@@ -81,6 +107,30 @@
     has_left = place > 0
     has_right = place < n_space - 1
 
+    arrivals = [
+        pltpu.make_async_copy(a, b, local_sem.at[i])
+        for i, (a, b) in enumerate(
+            [
+                (pre_in, pre),
+                (sat_in, sat),
+                (lp_in, lp),
+                (wells_in, wells),
+                (rate_in, rate),
+                (oi_in, oi),
+                (ow_in, ow),
+                (ov_in, ov),
+                (var_in, var),
+                (noise_in, noise),
+                (
+                    lp_in.at[:, :, pl.ds(pl.multiple_of(mem * part, part), part)],
+                    cols.at[pl.ds(mem * members, members)],
+                ),
+            ]
+        )
+    ]
+    for copy in arrivals:
+        copy.start()
+
     barrier = pltpu.get_barrier_semaphore()
     for d in range(1, n_mem):
         pl.semaphore_signal(
@@ -120,24 +170,26 @@
         row = width - 1 if side == 0 else 0
         target = right if side == 0 else left
         pairs = [
-            (pre.at[row], pre_ghost.at[side]),
-            (sat.at[row], sat_ghost.at[side]),
-            (lp.at[:, row], lp_ghost.at[side]),
+            (pre_in.at[row], pre_ghost.at[side]),
+            (sat_in.at[row], sat_ghost.at[side]),
+            (lp_in.at[:, row], lp_ghost.at[side]),
         ]
         return [
             remote(a, b, first_send.at[side, i], first_recv.at[side, i], target)
             for i, (a, b) in enumerate(pairs)
         ]
 
-    def halo(field, send, recv, k, m, side):
+    piece = yl // PARTS
+
+    def halo(field, send, recv, k, m, h, side):
         a = width if side == 0 else 1
         b = 0 if side == 0 else width + 1
-        rows = pl.ds(1, yl)
+        rows = pl.ds(1 + h * piece, piece)
         return remote(
             field.at[k, m, a, rows],
             field.at[k, m, b, rows],
-            send.at[k, m, side],
-            recv.at[k, m, side],
+            send.at[k, m, h, side],
+            recv.at[k, m, h, side],
             right if side == 0 else left,
         )
 
@@ -155,7 +207,7 @@
     def column(d):
         peer = lax.rem(mem + d, n_mem)
         return remote(
-            lp.at[:, :, pl.ds(pl.multiple_of(peer * part, part), part)],
+            lp_in.at[:, :, pl.ds(pl.multiple_of(peer * part, part), part)],
             cols.at[pl.ds(mem * members, members)],
             col_send.at[d],
             col_recv.at[d],
@@ -164,8 +216,8 @@
 
     for d in range(1, n_mem):
         column(d).start()
-    for m in range(members):
-        cols[mem * members + m] = lp[m, :, pl.ds(pl.multiple_of(mem * part, part), part)]
+    for copy in arrivals:
+        copy.wait()
 
     def strided(ref, lead, c):
         return ref[(*lead, pl.ds(c, SUB, stride=yl), slice(None))]
@@ -216,10 +268,13 @@
     well_y = jnp.floor((rest + 0.5) * (1.0 / nz))
     well_z = rest - well_y * nz
     count = well.shape[1]
-    pos = iota((ny, count), 0)
-    held_y = ((pos % SUB) * yl + pos // SUB).astype(jnp.float32)
-    at_z = as_float(pos.astype(jnp.float32) == well_z)
-    at_y = held_y == well_y
+
+    def held_y(lanes):
+        shape = (yl, SUB, lanes)
+        return (iota(shape, 1) * yl + iota(shape, 0)).astype(jnp.float32).reshape(ny, lanes)
+
+    at_z = as_float(iota((nz, count), 0).astype(jnp.float32) == well_z)
+    at_y = held_y(count) == well_y
     for r in range(width):
         here = well_x == (place * width + r).astype(jnp.float32)
         at_row = jnp.where(at_y & here, rate[...], 0.0)
@@ -228,82 +283,69 @@
         )
         src[r] = field.reshape(yl, SUB, nz)
 
-    def dot(a, b):
-        return jnp.dot(a, b, precision=HIGH, preferred_element_type=jnp.float32)
-
-    index_all = oi[...].astype(jnp.float32)
-    weight_all = ow[...]
-    from_obs = iota((nobs, row_taps), 0)
-    tap_lane = iota((nobs, row_taps), 1)
-    own_tap = iota((taps, row_taps), 0) == iota((taps, row_taps), 1) // per_row
-    tap_pos = iota((ny, row_taps), 0)
-    tap_y = ((tap_pos % SUB) * yl + tap_pos // SUB).astype(jnp.float32)
-    tap_z = tap_pos.astype(jnp.float32)
-    z_hot, y_hot, gather_taps = [], [], []
-    for r in range(width):
+    def tables(r):
         x = place * width + r
-        select = as_float(from_obs == x + total_rows * (tap_lane % per_row))
-        index = jnp.sum(jnp.where(own_tap, dot(index_all, select), 0.0), axis=0, keepdims=True)
-        weight = jnp.sum(jnp.where(own_tap, dot(weight_all, select), 0.0), axis=0, keepdims=True)
+        tap_lane = iota((1, row_taps), 1)
+        select = as_float(iota((nobs, row_taps), 0) == x + total_rows * (tap_lane % per_row))
+        both = jnp.concatenate([oi[...].astype(jnp.float32), ow[...]], axis=0)
+        found = split_dot(both, select)
+        own_tap = iota((taps, row_taps), 0) == tap_lane // per_row
+        index = jnp.sum(jnp.where(own_tap, found[:taps], 0.0), axis=0, keepdims=True)
+        weight = jnp.sum(jnp.where(own_tap, found[taps:], 0.0), axis=0, keepdims=True)
         rest = index - (x * plane).astype(jnp.float32)
         cell_y = jnp.floor((rest + 0.5) * (1.0 / nz))
         cell_z = rest - cell_y * nz
-        z_hot.append(as_float(tap_z == cell_z))
-        y_hot.append(jnp.where(tap_y == cell_y, weight, 0.0))
-        gather_taps.append(
-            as_float(
-                iota((row_taps, LANES), 1) == r * per_row + iota((row_taps, LANES), 0) % per_row
-            )
-        )
-    obs_lane = iota((nobs, LANES), 1)
-    own_obs = as_float(
-        (iota((nobs, LANES), 0) == place * width + obs_lane // per_row + total_rows * (obs_lane % per_row))
-        & (obs_lane < local_obs)
-    )
-    noise_own = dot(noise[...], own_obs)
-    value_own = dot(jnp.broadcast_to(ov[...], (SUB, nobs)), own_obs)
-    var_own = dot(jnp.broadcast_to(var[...], (SUB, nobs)), own_obs)
-
-    each(first, "wait_recv", False)
-    for side in (0, 1):
-        row = 0 if side == 0 else width + 1
-        there = as_float(has_left if side == 0 else has_right)
-        for c in range(yl):
-            s = strided(sat_ghost, (side,), c)
-            p = strided(pre_ghost, (side,), c)
-            for m in range(members):
-                half = 0.5 * there * jnp.exp(strided(lp_ghost, (side, m), c))
-                lam, frac = props(half, s)
-                half_perm[m, row, c] = half
-                L[0, m, row, c + 1] = lam
-                F[0, m, row, c + 1] = frac
-                Q[0, m, row, c + 1] = p
-
-    def beside(field, k, m, r, c):
-        mid = pl.ds(1 + c, CHUNK)
-        return [
-            field[k, m, r + 1, mid],
-            field[k, m, r - 1, mid],
-            field[k, m, r, pl.ds(c + 2, CHUNK)],
-            field[k, m, r, pl.ds(c, CHUNK)],
-        ]
-
-    def saturate(k, m, r):
-        for c in range(0, yl, CHUNK):
+        z_hot[r] = as_float(iota((nz, row_taps), 0).astype(jnp.float32) == cell_z)
+        y_hot[r] = jnp.where(held_y(row_taps) == cell_y, weight, 0.0)
+        tap_sum[r] = as_float(
+            iota((row_taps, LANES), 1) == r * per_row + iota((row_taps, 1), 0) % per_row
+        )
+
+    def own_data():
+        lane = iota((1, LANES), 1)
+        cell = place * width + lane // per_row + total_rows * (lane % per_row)
+        select = as_float(iota((nobs, LANES), 0) == jnp.where(lane < local_obs, cell, -1))
+        rows = [jnp.broadcast_to(ov[...], (SUB, nobs)), jnp.broadcast_to(var[...], (SUB, nobs))]
+        pad = jnp.zeros((16 - ens % 16, nobs), jnp.float32)
+        obs_own[...] = split_dot(jnp.concatenate(rows + [noise[...], pad], axis=0), select)
+
+    def first_ghosts():
+        each(first, "wait_recv", False)
+        for side in (0, 1):
+            row = 0 if side == 0 else width + 1
+            there = as_float(has_left if side == 0 else has_right)
+            for c in range(yl):
+                s = strided(sat_ghost, (side,), c)
+                p = strided(pre_ghost, (side,), c)
+                for m in range(members):
+                    half = 0.5 * there * jnp.exp(strided(lp_ghost, (side, m), c))
+                    lam, frac = props(half, s)
+                    half_perm[m, row, c] = half
+                    L[0, m, row, c + 1] = lam
+                    F[0, m, row, c + 1] = frac
+                    Q[0, m, row, c + 1] = p
+
+    def slab(field, k, m, r, c):
+        return field[k, m, r, pl.ds(c, CHUNK + 2)]
+
+    def saturate(k, m, r, lo, hi):
+        for c in range(lo, hi, CHUNK):
             mid = pl.ds(1 + c, CHUNK)
-            lam, frac, press = L[k, m, r, mid], F[k, m, r, mid], Q[k, m, r, mid]
+            lam_y, frac_y, press_y = slab(L, k, m, r, c), slab(F, k, m, r, c), slab(Q, k, m, r, c)
+            lam, frac, press = lam_y[1:-1], frac_y[1:-1], press_y[1:-1]
+            flux = (lam_y[:-1] + lam_y[1:]) * (press_y[:-1] - press_y[1:])
+            along = flux * jnp.where(flux > 0.0, frac_y[:-1], frac_y[1:])
+            outflow = along[1:] - along[:-1]
+            for row in (r - 1, r + 1):
+                flux = (lam + L[k, m, row, mid]) * (press - Q[k, m, row, mid])
+                outflow = outflow + flux * jnp.where(flux > 0.0, frac, F[k, m, row, mid])
             lam_next = pltpu.roll(lam, nz - 1, 2)
             frac_next = pltpu.roll(frac, nz - 1, 2)
             press_next = pltpu.roll(press, nz - 1, 2)
             flux = (lam + lam_next) * inner * (press - press_next)
             along = flux * jnp.where(flux > 0.0, frac, frac_next)
-            outflow = along - pltpu.roll(along, 1, 2)
+            outflow = outflow + (along - pltpu.roll(along, 1, 2))
             outflow = outflow + ends * jnp.maximum(lam * press, 0.0) * frac
-            for lam_j, frac_j, press_j in zip(
-                beside(L, k, m, r, c), beside(F, k, m, r, c), beside(Q, k, m, r, c)
-            ):
-                flux = (lam + lam_j) * (press - press_j)
-                outflow = outflow + flux * jnp.where(flux > 0.0, frac, frac_j)
             source = src[r - 1, pl.ds(c, CHUNK)]
             water = jnp.maximum(source, 0.0) + jnp.minimum(source, 0.0) * frac
             s = jnp.clip(S[k, m, r, mid] + time_step * (water - outflow), 0.0, 1.0)
@@ -311,87 +353,111 @@
             S[k + 1, m, r, mid] = s
             L[k + 1, m, r, mid] = lam
             F[k + 1, m, r, mid] = frac
+
+    def saturate_pads(k, m, r):
         pads(L, k + 1, m, r)
         pads(F, k + 1, m, r)
 
-    def pressure(k, m, r):
-        for c in range(0, yl, CHUNK):
+    def pressure(k, m, r, lo, hi):
+        for c in range(lo, hi, CHUNK):
             mid = pl.ds(1 + c, CHUNK)
-            lam, press = L[k + 1, m, r, mid], Q[k, m, r, mid]
-            lam_j = beside(L, k + 1, m, r, c) + [
-                pltpu.roll(lam, 1, 2) * not_first,
-                pltpu.roll(lam, nz - 1, 2) * inner,
-            ]
-            press_j = beside(Q, k, m, r, c) + [
-                pltpu.roll(press, 1, 2) * not_first,
-                pltpu.roll(press, nz - 1, 2) * inner,
-            ]
-            denom = 1.0 + 6.0 * lam + sum(lam_j[1:], lam_j[0])
-            numer = press + src[r - 1, pl.ds(c, CHUNK)] + lam * sum(press_j[1:], press_j[0])
-            for a, b in zip(lam_j, press_j):
+            lam_y, press_y = slab(L, k + 1, m, r, c), slab(Q, k, m, r, c)
+            both_y = lam_y * press_y
+            lam, press = lam_y[1:-1], press_y[1:-1]
+            numer = press + src[r - 1, pl.ds(c, CHUNK)] + both_y[2:] + both_y[:-2]
+            lam_sum = lam_y[2:] + lam_y[:-2]
+            press_sum = press_y[2:] + press_y[:-2]
+            others = [(L[k + 1, m, row, mid], Q[k, m, row, mid]) for row in (r - 1, r + 1)]
+            others.append((pltpu.roll(lam, 1, 2) * not_first, pltpu.roll(press, 1, 2) * not_first))
+            others.append((pltpu.roll(lam, nz - 1, 2) * inner, pltpu.roll(press, nz - 1, 2) * inner))
+            for a, b in others:
                 numer = numer + a * b
-            Q[k + 1, m, r, mid] = numer / denom
+                lam_sum = lam_sum + a
+                press_sum = press_sum + b
+            Q[k + 1, m, r, mid] = (numer + lam * press_sum) / (1.0 + 6.0 * lam + lam_sum)
+
+    def pressure_pads(k, m, r):
         pads(Q, k + 1, m, r)
 
-    def ghost_props(k, m, row):
-        for c in range(0, yl, CHUNK):
+    def ghost_props(k, m, row, lo, hi):
+        for c in range(lo, hi, CHUNK):
             mid = pl.ds(1 + c, CHUNK)
             lam, frac = props(half_perm[m, row, pl.ds(c, CHUNK)], S[k, m, row, mid])
             L[k, m, row, mid] = lam
             F[k, m, row, mid] = frac
 
-    def s_halo(k, m):
-        return lambda side: [halo(S, s_send, s_recv, k, m, side)]
-
-    def p_halo(k, m):
-        return lambda side: [halo(Q, p_send, p_recv, k, m, side)]
-
-    def inside(step, k, m):
+    def s_halo(k, m, h):
+        return lambda side: [halo(S, s_send, s_recv, k, m, h, side)]
+
+    def p_halo(k, m, h):
+        return lambda side: [halo(Q, p_send, p_recv, k, m, h, side)]
+
+    def inside(step, finish, k, m):
         @pl.loop(2, width)
         def _(r):
-            step(k, m, r)
-
-    def border(step, k, m):
+            step(k, m, r, 0, yl)
+            finish(k, m, r)
+
+    def border(step, finish, k, m, h):
         @pl.loop(0, 2)
         def _(i):
-            step(k, m, 1 + i * (width - 1))
+            r = 1 + i * (width - 1)
+            step(k, m, r, h * piece, (h + 1) * piece)
+            if h == PARTS - 1:
+                finish(k, m, r)
+
+    halves = [(m, h) for m in range(members) for h in range(PARTS)]
 
     @pl.loop(0, SWEEPS)
     def _(k):
         for m in range(members):
-            inside(saturate, k, m)
+            inside(saturate, saturate_pads, k, m)
+
+        @pl.when(k == 0)
+        def _():
+            first_ghosts()
+
+        for m, h in halves:
+
+            @pl.when(k > 0)
+            def _(m=m, h=h):
+                each(p_halo(k, m, h), "wait_recv", False)
+
+            border(saturate, saturate_pads, k, m, h)
+            each(s_halo(k + 1, m, h), "start", True)
         for m in range(members):
-
-            @pl.when(k > 0)
-            def _(m=m):
-                each(p_halo(k, m), "wait_recv", False)
-
-            border(saturate, k, m)
-            each(s_halo(k + 1, m), "start", True)
-        for m in range(members):
-            inside(pressure, k, m)
-        for m in range(members):
-            each(s_halo(k + 1, m), "wait_recv", False)
+            inside(pressure, pressure_pads, k, m)
+
+        @pl.when(k < width)
+        def _():
+            tables(k)
+
+        @pl.when(k == SWEEPS - 1)
+        def _():
+            own_data()
+
+        for m, h in halves:
+            each(s_halo(k + 1, m, h), "wait_recv", False)
 
             @pl.loop(0, 2)
-            def _(i, m=m):
-                ghost_props(k + 1, m, i * (width + 1))
-
-            border(pressure, k, m)
+            def _(i, m=m, h=h):
+                ghost_props(k + 1, m, i * (width + 1), h * piece, (h + 1) * piece)
+
+            border(pressure, pressure_pads, k, m, h)
 
             @pl.when(k + 1 < SWEEPS)
-            def _(m=m):
-                each(p_halo(k + 1, m), "start", True)
-
-    member_row = iota((ens, LANES), 0)
+            def _(m=m, h=h):
+                each(p_halo(k + 1, m, h), "start", True)
+
     own = jnp.zeros((ens, LANES), jnp.float32)
     for r in range(width):
         found = jnp.zeros((ens, row_taps), jnp.float32)
+        fields = Q[SWEEPS, :, r + 1, pl.ds(1, yl)].reshape(members * ny, nz)
+        columns = split_dot(fields, z_hot[r])
         for m in range(members):
-            field = Q[SWEEPS, m, r + 1, pl.ds(1, yl)].reshape(ny, nz)
-            picked = jnp.sum(dot(field, z_hot[r]) * y_hot[r], axis=0, keepdims=True)
+            picked = jnp.sum(columns[m * ny : (m + 1) * ny] * y_hot[r], axis=0, keepdims=True)
             found = jnp.where(iota((ens, row_taps), 0) == mem * members + m, picked, found)
-        own = own + dot(found, gather_taps[r])
+        own = own + split_dot(found, tap_sum[r])
     pred[mem] = own
 
     def share(d):
@@ -401,6 +467,8 @@
 
     for d in range(1, n_mem):
         share(d).start()
+    value_own, var_own = obs_own[:SUB], obs_own[SUB : 2 * SUB]
+    noise_own = obs_own[2 * SUB : 2 * SUB + ens]
     scale = jnp.where(iota((ens, LANES), 1) < local_obs, inflation * var_own, 1.0)
     inverse = jnp.where(iota((ens, LANES), 1) < local_obs, 1.0 / scale, 0.0)
     target_obs = value_own + jnp.sqrt(inflation * var_own) * noise_own
@@ -465,11 +533,12 @@
     @pl.loop(1, SWEEPS + 1)
     def _(k):
         for m in range(members):
-            each(s_halo(k, m), "wait_send", True)
-
-            @pl.when(k < SWEEPS)
-            def _(m=m):
-                each(p_halo(k, m), "wait_send", True)
+            for h in range(PARTS):
+                each(s_halo(k, m, h), "wait_send", True)
+
+                @pl.when(k < SWEEPS)
+                def _(m=m, h=h):
+                    each(p_halo(k, m, h), "wait_send", True)
 
 
 def body(
@@ -490,15 +559,34 @@
     ens = members * n_mem
     yl = ny // SUB
     part = ny // n_mem
+    row_taps = obs_index.size // (width * n_space)
+    operands = (
+        log_perm,
+        saturation,
+        pressure_init,
+        wells[None],
+        well_rate[None],
+        obs_index.T,
+        obs_weight.T,
+        obs_value[None],
+        obs_var[None],
+        noise,
+    )
     vmem = pl.BlockSpec(memory_space=pltpu.VMEM)
     state = pltpu.VMEM((SWEEPS + 1, members, width + 2, yl + 2, SUB, nz), jnp.float32)
     dma = pltpu.SemaphoreType.DMA
     return pl.pallas_call(
         functools.partial(kernel, n_mem, n_space),
         out_shape=jax.ShapeDtypeStruct((ens, width, part, nz), jnp.float32),
-        in_specs=[vmem] * 10,
+        in_specs=[pl.BlockSpec(memory_space=pltpu.HBM)] * 10,
         out_specs=vmem,
         scratch_shapes=[
+            *[pltpu.VMEM(a.shape, a.dtype) for a in operands],
+            pltpu.VMEM((width, nz, row_taps), jnp.float32),
+            pltpu.VMEM((width, ny, row_taps), jnp.float32),
+            pltpu.VMEM((width, row_taps, LANES), jnp.float32),
+            pltpu.VMEM((2 * SUB + 16, LANES), jnp.float32),
+            dma((11,)),
             state,
             state,
             state,
@@ -513,10 +601,10 @@
             pltpu.VMEM((n_space, ens, LANES), jnp.float32),
             dma((2, 3)),
             dma((2, 3)),
-            dma((SWEEPS + 1, members, 2)),
-            dma((SWEEPS + 1, members, 2)),
-            dma((SWEEPS + 1, members, 2)),
-            dma((SWEEPS + 1, members, 2)),
+            dma((SWEEPS + 1, members, PARTS, 2)),
+            dma((SWEEPS + 1, members, PARTS, 2)),
+            dma((SWEEPS + 1, members, PARTS, 2)),
+            dma((SWEEPS + 1, members, PARTS, 2)),
             dma((n_mem,)),
             dma((n_mem,)),
             dma((n_mem,)),
@@ -527,18 +615,7 @@
         compiler_params=pltpu.CompilerParams(
             collective_id=0, has_side_effects=True, vmem_limit_bytes=48 * 1024 * 1024
         ),
-    )(
-        log_perm,
-        saturation,
-        pressure_init,
-        wells[None],
-        well_rate[None],
-        obs_index.T,
-        obs_weight.T,
-        obs_value[None],
-        obs_var[None],
-        noise,
-    )
+    )(*operands)
 
 
 def solution(mesh):

time: 66.5 us -> 62.6 us (0.941)
  Pallas kernels: 59.5 us -> 55.6 us
    pallas_call x1, Pallas kernels: 59.5 us -> 55.6 us  [body(): pl.pallas_call(functools.partial(kernel, n_mem, n_space), out_shape=jax.S...]
where the time goes in v2:
time: 62.6 us; the launch traced here: 62.2 us
  Pallas kernels  55.6 us (89%)
  local copies, waits for them, and re-layouts  6.59 us (11%)
    pallas_call x1, Pallas kernels, body(): pl.pallas_call(functools.partial(kernel, n_mem, n_space), out_shape=jax.S...  55.6 us
    unnamed x21, local copies, waits for them, and re-layouts  6.59 us

profile of v2, /device:TPU:0, one launch (start us, length us, event | category | flops | bytes accessed | tf_op | source)
XLA Modules:
  0.0 62.2 jit_solution(16686510704910737368)
XLA Ops:
  0.0 0.0 copy-start.7
  0.0 0.0 copy-start.6
  0.0 0.0 copy-start.8
  0.0 0.0 copy-start.9
  0.0 0.7 %copy-done.7 = f32[512]{0:T(512)S(1)} copy-done((f32[512]{0:T(512)S(1)}, f32[512]{0:T(512)}, u32[]{:S(2)}) %copy-start.7) | copy-done | bytes 2072
  0.7 0.0 copy-done.6
  0.7 0.0 copy-done.8
  0.7 0.0 copy-done.9
  0.7 0.0 copy-start
  0.7 1.0 %copy-done = f32[2,4,128,128]{3,2,1,0:T(8,128)S(1)} copy-done((f32[2,4,128,128]{3,2,1,0:T(8,128)S(1)}, f32[2,4,128,128]{3,2,1,0:T(8,128)}, u32[]{:S(2)}) %copy-start) | copy-done | bytes 524312
  1.7 0.0 copy-start.1
  1.7 0.9 %copy-done.1 = f32[4,128,128]{2,1,0:T(8,128)S(1)} copy-done((f32[4,128,128]{2,1,0:T(8,128)S(1)}, f32[4,128,128]{2,1,0:T(8,128)}, u32[]{:S(2)}) %copy-start.1) | copy-done | bytes 262168
  2.7 0.0 copy-start.2
  2.7 0.9 %copy-done.2 = f32[4,128,128]{2,1,0:T(8,128)S(1)} copy-done((f32[4,128,128]{2,1,0:T(8,128)S(1)}, f32[4,128,128]{2,1,0:T(8,128)}, u32[]{:S(2)}) %copy-start.2) | copy-done | bytes 262168
  3.6 0.0 copy-start.3
  3.6 0.7 %copy-done.3 = s32[512,8]{0,1:T(8,128)S(1)} copy-done((s32[512,8]{0,1:T(8,128)S(1)}, s32[512,8]{0,1:T(8,128)}, u32[]{:S(2)}) %copy-start.3) | copy-done | bytes 16408
  4.4 0.0 copy-start.4
  4.4 0.7 %copy-done.4 = f32[512,8]{0,1:T(8,128)S(1)} copy-done((f32[512,8]{0,1:T(8,128)S(1)}, f32[512,8]{0,1:T(8,128)}, u32[]{:S(2)}) %copy-start.4) | copy-done | bytes 16408
  5.1 0.0 copy-start.5
  5.1 0.7 %copy-done.5 = f32[8,512]{1,0:T(8,128)S(1)} copy-done((f32[8,512]{1,0:T(8,128)S(1)}, f32[8,512]{1,0:T(8,128)}, u32[]{:S(2)}) %copy-start.5) | copy-done | bytes 16408
  5.8 55.6 %shard_map.100 = f32[8,4,32,128]{3,2,1,0:T(8,128)S(1)} custom-call(f32[2,4,128,128]{3,2,1,0:T(8,128)S(1)} %copy-done, f32[4,128,128]{2,1,0:T(8,128)S(1)} %copy-done.1, f32[4,128,128]{2,1,0:T(8,128)S(1)} %copy-done.2, s32[1,64]{1,0:T(1,128)S(1)} %bitcast.10, f32[1,64]{1,0:T(1,128)S(1)} %bitcast.11, s32[8,512]{1,0:T(8,128)S(1)} %bitcast.6, ...), custom_call_target="tpu_custom_call" | custom-call | tf_op jit(solution)/shard_map/pallas_call | solution.py:578
  61.4 0.8 %copy.12 = f32[8,4,32,128]{3,2,1,0:T(8,128)} copy(f32[8,4,32,128]{3,2,1,0:T(8,128)S(1)} %shard_map.100) | data formatting | bytes 1048576
Async XLA Ops:
  0.0 0.7 %copy-start.7 = (f32[512]{0:T(512)S(1)}, f32[512]{0:T(512)}, u32[]{:S(2)}) copy-start(f32[512]{0:T(512)} %param.18) | copy-start | bytes 6148
  0.0 0.7 %copy-start.6 = (f32[512]{0:T(512)S(1)}, f32[512]{0:T(512)}, u32[]{:S(2)}) copy-start(f32[512]{0:T(512)} %param.17) | copy-start | bytes 6148
  0.0 0.7 %copy-start.8 = (s32[64]{0:T(128)S(1)}, s32[64]{0:T(128)}, u32[]{:S(2)}) copy-start(s32[64]{0:T(128)} %param.13) | copy-start | bytes 772
  0.0 0.7 %copy-start.9 = (f32[64]{0:T(128)S(1)}, f32[64]{0:T(128)}, u32[]{:S(2)}) copy-start(f32[64]{0:T(128)} %param.14) | copy-start | bytes 772
  0.7 1.0 %copy-start = (f32[2,4,128,128]{3,2,1,0:T(8,128)S(1)}, f32[2,4,128,128]{3,2,1,0:T(8,128)}, u32[]{:S(2)}) copy-start(f32[2,4,128,128]{3,2,1,0:T(8,128)} %lp_in.1) | copy-start | bytes 1572868
  1.7 0.9 %copy-start.1 = (f32[4,128,128]{2,1,0:T(8,128)S(1)}, f32[4,128,128]{2,1,0:T(8,128)}, u32[]{:S(2)}) copy-start(f32[4,128,128]{2,1,0:T(8,128)} %sat_in.1) | copy-start | bytes 786436
  2.7 0.9 %copy-start.2 = (f32[4,128,128]{2,1,0:T(8,128)S(1)}, f32[4,128,128]{2,1,0:T(8,128)}, u32[]{:S(2)}) copy-start(f32[4,128,128]{2,1,0:T(8,128)} %pre_in.1) | copy-start | bytes 786436
  3.6 0.7 %copy-start.3 = (s32[512,8]{0,1:T(8,128)S(1)}, s32[512,8]{0,1:T(8,128)}, u32[]{:S(2)}) copy-start(s32[512,8]{0,1:T(8,128)} %param.15) | copy-start | bytes 49156
  4.4 0.7 %copy-start.4 = (f32[512,8]{0,1:T(8,128)S(1)}, f32[512,8]{0,1:T(8,128)}, u32[]{:S(2)}) copy-start(f32[512,8]{0,1:T(8,128)} %param.16) | copy-start | bytes 49156
  5.1 0.7 %copy-start.5 = (f32[8,512]{1,0:T(8,128)S(1)}, f32[8,512]{1,0:T(8,128)}, u32[]{:S(2)}) copy-start(f32[8,512]{1,0:T(8,128)} %noise_in.1) | copy-start | bytes 49156

commit v3 on v2

--- a/solution.py
+++ b/solution.py
@@ -25,6 +25,11 @@
 
 def as_float(cond):
     return jnp.where(cond, 1.0, 0.0).astype(jnp.float32)
+
+
+def inverse_of(x):
+    r = pl.reciprocal(x, approx=True)
+    return r * (2.0 - x * r)
 
 
 def split_dot(a, hot):
@@ -72,6 +77,8 @@
     Q,
     half_perm,
     src,
+    faces,
+    picks,
     lp_ghost,
     sat_ghost,
     pre_ghost,
@@ -226,7 +233,7 @@
         water = s * s
         dry = 1.0 - s
         total = water + dry * dry * 0.25
-        return half * total, water / total
+        return half * total, water * inverse_of(total)
 
     sub = iota((SUB, nz), 0)
     lane = iota((SUB, nz), 1)
@@ -242,25 +249,23 @@
         bottom = field[k, m, r, 1]
         field[k, m, r, yl + 1] = jnp.where(sub_last, 0.0, pltpu.roll(bottom, SUB - 1, 0))
 
-    def load_row(m, r):
+    @pl.loop(0, width)
+    def _(r):
         for c in range(yl):
-            half = 0.5 * jnp.exp(strided(lp, (m, r), c))
             s = strided(sat, (r,), c)
-            lam, frac = props(half, s)
-            half_perm[m, r + 1, c] = half
-            S[0, m, r + 1, c + 1] = s
-            L[0, m, r + 1, c + 1] = lam
-            F[0, m, r + 1, c + 1] = frac
-            Q[0, m, r + 1, c + 1] = strided(pre, (r,), c)
-        pads(L, 0, m, r + 1)
-        pads(F, 0, m, r + 1)
-        pads(Q, 0, m, r + 1)
-
-    for m in range(members):
-
-        @pl.loop(0, width)
-        def _(r, m=m):
-            load_row(m, r)
+            press = strided(pre, (r,), c)
+            for m in range(members):
+                half = 0.5 * jnp.exp(strided(lp, (m, r), c))
+                lam, frac = props(half, s)
+                half_perm[m, r + 1, c] = half
+                S[0, m, r + 1, c + 1] = s
+                L[0, m, r + 1, c + 1] = lam
+                F[0, m, r + 1, c + 1] = frac
+                Q[0, m, r + 1, c + 1] = press
+        for m in range(members):
+            pads(L, 0, m, r + 1)
+            pads(F, 0, m, r + 1)
+            pads(Q, 0, m, r + 1)
 
     well = wells[...].astype(jnp.float32)
     well_x = jnp.floor((well + 0.5) * (1.0 / plane))
@@ -328,7 +333,11 @@
     def slab(field, k, m, r, c):
         return field[k, m, r, pl.ds(c, CHUNK + 2)]
 
-    def saturate(k, m, r, lo, hi):
+    def face(k, m, r, mid):
+        flux = (L[k, m, r, mid] + L[k, m, r + 1, mid]) * (Q[k, m, r, mid] - Q[k, m, r + 1, mid])
+        return flux * jnp.where(flux > 0.0, F[k, m, r, mid], F[k, m, r + 1, mid])
+
+    def saturate(k, m, r, lo, hi, new_below, new_above, keep):
         for c in range(lo, hi, CHUNK):
             mid = pl.ds(1 + c, CHUNK)
             lam_y, frac_y, press_y = slab(L, k, m, r, c), slab(F, k, m, r, c), slab(Q, k, m, r, c)
@@ -336,9 +345,14 @@
             flux = (lam_y[:-1] + lam_y[1:]) * (press_y[:-1] - press_y[1:])
             along = flux * jnp.where(flux > 0.0, frac_y[:-1], frac_y[1:])
             outflow = along[1:] - along[:-1]
-            for row in (r - 1, r + 1):
-                flux = (lam + L[k, m, row, mid]) * (press - Q[k, m, row, mid])
-                outflow = outflow + flux * jnp.where(flux > 0.0, frac, F[k, m, row, mid])
+            here = pl.ds(c, CHUNK)
+            below = face(k, m, r - 1, mid) if new_below else faces[m, r - 1, here]
+            above = face(k, m, r, mid) if new_above else faces[m, r, here]
+            if keep and new_below:
+                faces[m, r - 1, here] = below
+            if keep and new_above:
+                faces[m, r, here] = above
+            outflow = outflow + (above - below)
             lam_next = pltpu.roll(lam, nz - 1, 2)
             frac_next = pltpu.roll(frac, nz - 1, 2)
             press_next = pltpu.roll(press, nz - 1, 2)
@@ -374,7 +388,9 @@
                 numer = numer + a * b
                 lam_sum = lam_sum + a
                 press_sum = press_sum + b
-            Q[k + 1, m, r, mid] = (numer + lam * press_sum) / (1.0 + 6.0 * lam + lam_sum)
+            Q[k + 1, m, r, mid] = (numer + lam * press_sum) * inverse_of(
+                1.0 + 6.0 * lam + lam_sum
+            )
 
     def pressure_pads(k, m, r):
         pads(Q, k + 1, m, r)
@@ -392,26 +408,54 @@
     def p_halo(k, m, h):
         return lambda side: [halo(Q, p_send, p_recv, k, m, h, side)]
 
-    def inside(step, finish, k, m):
+    def saturate_inside(k, m):
+        saturate(k, m, 2, 0, yl, True, True, True)
+        saturate_pads(k, m, 2)
+
+        @pl.loop(3, width)
+        def _(r):
+            saturate(k, m, r, 0, yl, False, True, True)
+            saturate_pads(k, m, r)
+
+    def saturate_border(k, m, h):
+        saturate(k, m, 1, h * piece, (h + 1) * piece, True, False, False)
+        saturate(k, m, width, h * piece, (h + 1) * piece, False, True, False)
+        if h == PARTS - 1:
+            saturate_pads(k, m, 1)
+            saturate_pads(k, m, width)
+
+    def pressure_inside(k, m):
         @pl.loop(2, width)
         def _(r):
-            step(k, m, r, 0, yl)
-            finish(k, m, r)
-
-    def border(step, finish, k, m, h):
+            pressure(k, m, r, 0, yl)
+            pressure_pads(k, m, r)
+
+    def pressure_border(k, m, h):
         @pl.loop(0, 2)
         def _(i):
             r = 1 + i * (width - 1)
-            step(k, m, r, h * piece, (h + 1) * piece)
+            pressure(k, m, r, h * piece, (h + 1) * piece)
             if h == PARTS - 1:
-                finish(k, m, r)
+                pressure_pads(k, m, r)
+
+    def picked_rows(some):
+        own = jnp.zeros((ens, LANES), jnp.float32)
+        for r in some:
+            found = jnp.zeros((ens, row_taps), jnp.float32)
+            fields = Q[SWEEPS, :, r + 1, pl.ds(1, yl)].reshape(members * ny, nz)
+            columns = split_dot(fields, z_hot[r])
+            for m in range(members):
+                picked = jnp.sum(columns[m * ny : (m + 1) * ny] * y_hot[r], axis=0, keepdims=True)
+                found = jnp.where(iota((ens, row_taps), 0) == mem * members + m, picked, found)
+            own = own + split_dot(found, tap_sum[r])
+        return own
 
     halves = [(m, h) for m in range(members) for h in range(PARTS)]
 
     @pl.loop(0, SWEEPS)
     def _(k):
         for m in range(members):
-            inside(saturate, saturate_pads, k, m)
+            saturate_inside(k, m)
 
         @pl.when(k == 0)
         def _():
@@ -423,10 +467,10 @@
             def _(m=m, h=h):
                 each(p_halo(k, m, h), "wait_recv", False)
 
-            border(saturate, saturate_pads, k, m, h)
+            saturate_border(k, m, h)
             each(s_halo(k + 1, m, h), "start", True)
         for m in range(members):
-            inside(pressure, pressure_pads, k, m)
+            pressure_inside(k, m)
 
         @pl.when(k < width)
         def _():
@@ -435,6 +479,7 @@
         @pl.when(k == SWEEPS - 1)
         def _():
             own_data()
+            picks[...] = picked_rows(range(1, width - 1))
 
         for m, h in halves:
             each(s_halo(k + 1, m, h), "wait_recv", False)
@@ -443,22 +488,13 @@
             def _(i, m=m, h=h):
                 ghost_props(k + 1, m, i * (width + 1), h * piece, (h + 1) * piece)
 
-            border(pressure, pressure_pads, k, m, h)
+            pressure_border(k, m, h)
 
             @pl.when(k + 1 < SWEEPS)
             def _(m=m, h=h):
                 each(p_halo(k + 1, m, h), "start", True)
 
-    own = jnp.zeros((ens, LANES), jnp.float32)
-    for r in range(width):
-        found = jnp.zeros((ens, row_taps), jnp.float32)
-        fields = Q[SWEEPS, :, r + 1, pl.ds(1, yl)].reshape(members * ny, nz)
-        columns = split_dot(fields, z_hot[r])
-        for m in range(members):
-            picked = jnp.sum(columns[m * ny : (m + 1) * ny] * y_hot[r], axis=0, keepdims=True)
-            found = jnp.where(iota((ens, row_taps), 0) == mem * members + m, picked, found)
-        own = own + split_dot(found, tap_sum[r])
-    pred[mem] = own
+    pred[mem] = picks[...] + picked_rows((0, width - 1))
 
     def share(d):
         return remote(
@@ -495,10 +531,26 @@
 
     for d in range(1, n_space):
         sum_part(d).start()
+    each(first, "wait_send", True)
+    for d in range(1, n_mem):
+        column(d).wait_send()
+        share(d).wait_send()
+
+    @pl.loop(1, SWEEPS + 1)
+    def _(k):
+        for m in range(members):
+            for h in range(PARTS):
+                each(s_halo(k, m, h), "wait_send", True)
+
+                @pl.when(k < SWEEPS)
+                def _(m=m, h=h):
+                    each(p_halo(k, m, h), "wait_send", True)
     for d in range(1, n_mem):
         column(d).wait_recv()
     for d in range(1, n_space):
         sum_part(d).wait_recv()
+    for d in range(1, n_space):
+        sum_part(d).wait_send()
     whole = gram[0]
     for a in range(1, n_space):
         whole = whole + gram[a]
@@ -522,23 +574,6 @@
                 for j in range(1, ens):
                     total = total + factors[j] * cols[j, r, pl.ds(c, SUB)]
                 out[m, r, pl.ds(c, SUB)] = total
-
-    each(first, "wait_send", True)
-    for d in range(1, n_mem):
-        column(d).wait_send()
-        share(d).wait_send()
-    for d in range(1, n_space):
-        sum_part(d).wait_send()
-
-    @pl.loop(1, SWEEPS + 1)
-    def _(k):
-        for m in range(members):
-            for h in range(PARTS):
-                each(s_halo(k, m, h), "wait_send", True)
-
-                @pl.when(k < SWEEPS)
-                def _(m=m, h=h):
-                    each(p_halo(k, m, h), "wait_send", True)
 
 
 def body(
@@ -593,6 +628,8 @@
             state,
             pltpu.VMEM((members, width + 2, yl, SUB, nz), jnp.float32),
             pltpu.VMEM((width, yl, SUB, nz), jnp.float32),
+            pltpu.VMEM((members, width, yl, SUB, nz), jnp.float32),
+            pltpu.VMEM((ens, LANES), jnp.float32),
             pltpu.VMEM((2, members, ny, nz), jnp.float32),
             pltpu.VMEM((2, ny, nz), jnp.float32),
             pltpu.VMEM((2, ny, nz), jnp.float32),
@@ -613,7 +650,7 @@
             dma((n_space,)),
         ],
         compiler_params=pltpu.CompilerParams(
-            collective_id=0, has_side_effects=True, vmem_limit_bytes=48 * 1024 * 1024
+            collective_id=0, has_side_effects=True, vmem_limit_bytes=62 * 1024 * 1024
         ),
     )(*operands)
 

time: 62.6 us -> 56.8 us (0.907)
  local copies, waits for them, and re-layouts: 6.59 us -> 1.87 us
  Pallas kernels: 55.6 us -> 54.8 us
    unnamed x21 -> x1, local copies, waits for them, and re-layouts: 6.59 us -> 1.87 us
    pallas_call x1, Pallas kernels: 55.6 us -> 54.8 us  [body(): pl.pallas_call(functools.partial(kernel, n_mem, n_space), out_shape=jax.S...]
where the time goes in v3:
time: 56.8 us; the launch traced here: 56.7 us
  Pallas kernels  54.8 us (96%)
  local copies, waits for them, and re-layouts  1.87 us (3%)
    pallas_call x1, Pallas kernels, body(): pl.pallas_call(functools.partial(kernel, n_mem, n_space), out_shape=jax.S...  54.8 us
    unnamed x1, local copies, waits for them, and re-layouts  1.87 us

profile of v3, /device:TPU:0, one launch (start us, length us, event | category | flops | bytes accessed | tf_op | source)
XLA Modules:
  0.0 56.7 jit_solution(11804725558073708528)
XLA Ops:
  0.0 54.8 %shard_map.100 = f32[8,4,32,128]{3,2,1,0:T(8,128)} custom-call(f32[2,4,128,128]{3,2,1,0:T(8,128)} %lp_in.1, f32[4,128,128]{2,1,0:T(8,128)} %sat_in.1, f32[4,128,128]{2,1,0:T(8,128)} %pre_in.1, s32[1,64]{1,0:T(1,128)} %bitcast.10, f32[1,64]{1,0:T(1,128)} %bitcast.11, s32[8,512]{1,0:T(8,128)} %bitcast.6, f32[8,512]{1,0:T(8,128)} %bitcast.7, f32[1,512]{1,0:T(1,128)} %bitcast.8, ...), custom_call_target="tpu_custom_call" | custom-call | tf_op jit(solution)/shard_map/pallas_call | solution.py:613
  54.8 1.9 %copy.12 = f32[8,4,32,128]{3,2,1,0:T(8,128)} copy(f32[8,4,32,128]{3,2,1,0:T(8,128)} %shard_map.100) | data formatting | bytes 1048576

commit v4 on v3

--- a/solution.py
+++ b/solution.py
@@ -55,7 +55,8 @@
     ov_in,
     var_in,
     noise_in,
-    out,
+    cols,
+    mixing,
     lp,
     sat,
     pre,
@@ -82,7 +83,6 @@
     lp_ghost,
     sat_ghost,
     pre_ghost,
-    cols,
     pred,
     gram,
     first_send,
@@ -450,26 +450,21 @@
             own = own + split_dot(found, tap_sum[r])
         return own
 
-    halves = [(m, h) for m in range(members) for h in range(PARTS)]
+    for m in range(members):
+        saturate_inside(0, m)
+    first_ghosts()
 
     @pl.loop(0, SWEEPS)
     def _(k):
         for m in range(members):
-            saturate_inside(k, m)
-
-        @pl.when(k == 0)
-        def _():
-            first_ghosts()
-
-        for m, h in halves:
-
-            @pl.when(k > 0)
-            def _(m=m, h=h):
-                each(p_halo(k, m, h), "wait_recv", False)
-
-            saturate_border(k, m, h)
-            each(s_halo(k + 1, m, h), "start", True)
-        for m in range(members):
+            for h in range(PARTS):
+
+                @pl.when(k > 0)
+                def _(m=m, h=h):
+                    each(p_halo(k, m, h), "wait_recv", False)
+
+                saturate_border(k, m, h)
+                each(s_halo(k + 1, m, h), "start", True)
             pressure_inside(k, m)
 
         @pl.when(k < width)
@@ -481,18 +476,23 @@
             own_data()
             picks[...] = picked_rows(range(1, width - 1))
 
-        for m, h in halves:
-            each(s_halo(k + 1, m, h), "wait_recv", False)
-
-            @pl.loop(0, 2)
-            def _(i, m=m, h=h):
-                ghost_props(k + 1, m, i * (width + 1), h * piece, (h + 1) * piece)
-
-            pressure_border(k, m, h)
+        for m in range(members):
+            for h in range(PARTS):
+                each(s_halo(k + 1, m, h), "wait_recv", False)
+
+                @pl.loop(0, 2)
+                def _(i, m=m, h=h):
+                    ghost_props(k + 1, m, i * (width + 1), h * piece, (h + 1) * piece)
+
+                pressure_border(k, m, h)
+
+                @pl.when(k + 1 < SWEEPS)
+                def _(m=m, h=h):
+                    each(p_halo(k + 1, m, h), "start", True)
 
             @pl.when(k + 1 < SWEEPS)
-            def _(m=m, h=h):
-                each(p_halo(k + 1, m, h), "start", True)
+            def _(m=m):
+                saturate_inside(k + 1, m)
 
     pred[mem] = picks[...] + picked_rows((0, width - 1))
 
@@ -561,19 +561,27 @@
     for i in range(ens):
         pivot_row = table[i : i + 1, :] / table[i : i + 1, i : i + 1]
         table = jnp.where(row_id == i, pivot_row, table - table[:, i : i + 1] * pivot_row)
-    mixing = (
+    mixing[...] = (
         table - jnp.mean(table, axis=0, keepdims=True) + as_float(row_id + ens == lane_id)
     )
-    for m in range(ens):
-        factors = [
-            jnp.broadcast_to(mixing[j : j + 1, ens + m : ens + m + 1], (SUB, nz)) for j in range(ens)
+
+
+def mix_kernel(mixing, cols, out):
+    ens, _, part, nz = cols.shape
+    factors = [
+        [
+            jnp.broadcast_to(mixing[j : j + 1, ens + m : ens + m + 1], (SUB, nz))
+            for j in range(ens)
         ]
-        for r in range(width):
-            for c in range(0, part, SUB):
-                total = factors[0] * cols[0, r, pl.ds(c, SUB)]
-                for j in range(1, ens):
-                    total = total + factors[j] * cols[j, r, pl.ds(c, SUB)]
-                out[m, r, pl.ds(c, SUB)] = total
+        for m in range(ens)
+    ]
+    for c in range(0, part, SUB):
+        rows = [cols[j, 0, pl.ds(c, SUB)] for j in range(ens)]
+        for m in range(ens):
+            total = factors[m][0] * rows[0]
+            for j in range(1, ens):
+                total = total + factors[m][j] * rows[j]
+            out[m, 0, pl.ds(c, SUB)] = total
 
 
 def body(
@@ -610,11 +618,12 @@
     vmem = pl.BlockSpec(memory_space=pltpu.VMEM)
     state = pltpu.VMEM((SWEEPS + 1, members, width + 2, yl + 2, SUB, nz), jnp.float32)
     dma = pltpu.SemaphoreType.DMA
-    return pl.pallas_call(
+    columns = jax.ShapeDtypeStruct((ens, width, part, nz), jnp.float32)
+    cols, mixing = pl.pallas_call(
         functools.partial(kernel, n_mem, n_space),
-        out_shape=jax.ShapeDtypeStruct((ens, width, part, nz), jnp.float32),
+        out_shape=(columns, jax.ShapeDtypeStruct((ens, LANES), jnp.float32)),
         in_specs=[pl.BlockSpec(memory_space=pltpu.HBM)] * 10,
-        out_specs=vmem,
+        out_specs=(pl.BlockSpec(memory_space=pltpu.HBM), vmem),
         scratch_shapes=[
             *[pltpu.VMEM(a.shape, a.dtype) for a in operands],
             pltpu.VMEM((width, nz, row_taps), jnp.float32),
@@ -633,7 +642,6 @@
             pltpu.VMEM((2, members, ny, nz), jnp.float32),
             pltpu.VMEM((2, ny, nz), jnp.float32),
             pltpu.VMEM((2, ny, nz), jnp.float32),
-            pltpu.VMEM((ens, width, part, nz), jnp.float32),
             pltpu.VMEM((n_mem, ens, LANES), jnp.float32),
             pltpu.VMEM((n_space, ens, LANES), jnp.float32),
             dma((2, 3)),
@@ -653,6 +661,15 @@
             collective_id=0, has_side_effects=True, vmem_limit_bytes=62 * 1024 * 1024
         ),
     )(*operands)
+    block = pl.BlockSpec((ens, 1, part, nz), lambda r: (0, r, 0, 0))
+    return pl.pallas_call(
+        mix_kernel,
+        grid=(width,),
+        out_shape=columns,
+        in_specs=[pl.BlockSpec((ens, LANES), lambda r: (0, 0)), block],
+        out_specs=block,
+        compiler_params=pltpu.CompilerParams(vmem_limit_bytes=62 * 1024 * 1024),
+    )(mixing, cols)
 
 
 def solution(mesh):

time: 56.8 us -> 58.3 us (1.026)
  Pallas kernels: 54.8 us -> 58.1 us
  local copies, waits for them, and re-layouts: 1.87 us -> 0 us
    pallas_call x1 -> x2, Pallas kernels: 54.8 us -> 58.1 us  [the longest x1 54.6 us: body(): pl.pallas_call(functools.partial(kernel, n_mem, n_space), out_shape=(colu...]
    unnamed x1 -> x0, local copies, waits for them, and re-layouts: 1.87 us -> none
where the time goes in v4:
time: 58.3 us; the launch traced here: 58.2 us
  Pallas kernels  58.1 us (100%)
    pallas_call x1, Pallas kernels, body(): pl.pallas_call(functools.partial(kernel, n_mem, n_space), out_shape=(colu...  54.6 us
    pallas_call x1, Pallas kernels, body(): pl.pallas_call(mix_kernel, grid=(width,), out_shape=columns, in_specs=[pl...  3.54 us

profile of v4, /device:TPU:0, one launch (start us, length us, event | category | flops | bytes accessed | tf_op | source)
XLA Modules:
  0.0 58.2 jit_solution(16406796785537533811)
XLA Ops:
  0.0 54.6 %shard_map.100 = (f32[8,4,32,128]{3,2,1,0:T(8,128)}, f32[8,128]{1,0:T(8,128)}) custom-call(f32[2,4,128,128]{3,2,1,0:T(8,128)} %lp_in.1, f32[4,128,128]{2,1,0:T(8,128)} %sat_in.1, f32[4,128,128]{2,1,0:T(8,128)} %pre_in.1, s32[1,64]{1,0:T(1,128)} %bitcast.10, f32[1,64]{1,0:T(1,128)} %bitcast.11, s32[8,512]{1,0:T(8,128)} %bitcast.6, f32[8,512]{1,0:T(8,128)} %bitcast.7, ...), custom_call_target="tpu_custom_call" | custom-call | tf_op jit(solution)/shard_map/pallas_call | solution.py:622
  54.6 3.5 %shard_map.101 = f32[8,4,32,128]{3,2,1,0:T(8,128)} custom-call(f32[8,128]{1,0:T(8,128)} %get-tuple-element.7.mixing, f32[8,4,32,128]{3,2,1,0:T(8,128)} %get-tuple-element.8.cols), custom_call_target="tpu_custom_call" | custom-call | tf_op jit(solution)/shard_map/pallas_call | solution.py:665

commit v5 on v3

--- a/solution.py
+++ b/solution.py
@@ -15,8 +15,8 @@
 HIGH = lax.Precision.HIGHEST
 SUB = 8
 LANES = 128
-CHUNK = 4
-PARTS = 2
+CHUNK = 8
+PARTS = 1
 
 
 def iota(shape, dim):
@@ -450,26 +450,21 @@
             own = own + split_dot(found, tap_sum[r])
         return own
 
-    halves = [(m, h) for m in range(members) for h in range(PARTS)]
+    for m in range(members):
+        saturate_inside(0, m)
+    first_ghosts()
 
     @pl.loop(0, SWEEPS)
     def _(k):
         for m in range(members):
-            saturate_inside(k, m)
-
-        @pl.when(k == 0)
-        def _():
-            first_ghosts()
-
-        for m, h in halves:
-
-            @pl.when(k > 0)
-            def _(m=m, h=h):
-                each(p_halo(k, m, h), "wait_recv", False)
-
-            saturate_border(k, m, h)
-            each(s_halo(k + 1, m, h), "start", True)
-        for m in range(members):
+            for h in range(PARTS):
+
+                @pl.when(k > 0)
+                def _(m=m, h=h):
+                    each(p_halo(k, m, h), "wait_recv", False)
+
+                saturate_border(k, m, h)
+                each(s_halo(k + 1, m, h), "start", True)
             pressure_inside(k, m)
 
         @pl.when(k < width)
@@ -481,18 +476,23 @@
             own_data()
             picks[...] = picked_rows(range(1, width - 1))
 
-        for m, h in halves:
-            each(s_halo(k + 1, m, h), "wait_recv", False)
-
-            @pl.loop(0, 2)
-            def _(i, m=m, h=h):
-                ghost_props(k + 1, m, i * (width + 1), h * piece, (h + 1) * piece)
-
-            pressure_border(k, m, h)
+        for m in range(members):
+            for h in range(PARTS):
+                each(s_halo(k + 1, m, h), "wait_recv", False)
+
+                @pl.loop(0, 2)
+                def _(i, m=m, h=h):
+                    ghost_props(k + 1, m, i * (width + 1), h * piece, (h + 1) * piece)
+
+                pressure_border(k, m, h)
+
+                @pl.when(k + 1 < SWEEPS)
+                def _(m=m, h=h):
+                    each(p_halo(k + 1, m, h), "start", True)
 
             @pl.when(k + 1 < SWEEPS)
-            def _(m=m, h=h):
-                each(p_halo(k + 1, m, h), "start", True)
+            def _(m=m):
+                saturate_inside(k + 1, m)
 
     pred[mem] = picks[...] + picked_rows((0, width - 1))
 

time: 56.8 us -> 60.3 us (1.062)
  Pallas kernels: 54.8 us -> 58.3 us
    pallas_call x1, Pallas kernels: 54.8 us -> 58.3 us  [body(): pl.pallas_call(functools.partial(kernel, n_mem, n_space), out_shape=jax.S...]
where the time goes in v5:
time: 60.3 us; the launch traced here: 60.2 us
  Pallas kernels  58.3 us (97%)
  local copies, waits for them, and re-layouts  1.87 us (3%)
    pallas_call x1, Pallas kernels, body(): pl.pallas_call(functools.partial(kernel, n_mem, n_space), out_shape=jax.S...  58.3 us
    unnamed x1, local copies, waits for them, and re-layouts  1.87 us

profile of v5, /device:TPU:0, one launch (start us, length us, event | category | flops | bytes accessed | tf_op | source)
XLA Modules:
  0.0 60.2 jit_solution(2994888326061529057)
XLA Ops:
  0.0 58.3 %shard_map.100 = f32[8,4,32,128]{3,2,1,0:T(8,128)} custom-call(f32[2,4,128,128]{3,2,1,0:T(8,128)} %lp_in.1, f32[4,128,128]{2,1,0:T(8,128)} %sat_in.1, f32[4,128,128]{2,1,0:T(8,128)} %pre_in.1, s32[1,64]{1,0:T(1,128)} %bitcast.10, f32[1,64]{1,0:T(1,128)} %bitcast.11, s32[8,512]{1,0:T(8,128)} %bitcast.6, f32[8,512]{1,0:T(8,128)} %bitcast.7, f32[1,512]{1,0:T(1,128)} %bitcast.8, ...), custom_call_target="tpu_custom_call" | custom-call | tf_op jit(solution)/shard_map/pallas_call | solution.py:613
  58.3 1.9 %copy.12 = f32[8,4,32,128]{3,2,1,0:T(8,128)} copy(f32[8,4,32,128]{3,2,1,0:T(8,128)} %shard_map.100) | data formatting | bytes 1048576
